TPU v7x, 256 devices: a whole 4x4x8 slice. The times are simulated.
256 devices in a mesh: dp: 64 (over y, z, core), mp: 4 (over x).
Axes of the slice: x: 4, y: 4, z: 8, core: 2. Of those that a mesh axis runs over, the one named last changes fastest.
Arguments:
- pixels: bfloat16 [9216, 588], P('dp'), may hold values from -40 to 40
- patch_counts: int32 [192], P('dp'), may hold values from 12 to 48, as said below
- pack_index: int32 [192], P('dp'), may hold values from 0 to 63, as said below
- embed_weight: bfloat16 [588, 4, 1536], P(None, 'mp', 'dp'), may hold values from -1 to 1
- norm_gain: float32 [6144], P('mp'), may hold values from 0.5 to 1.5
- query_weight: bfloat16 [6144, 3072], P('dp', 'mp'), may hold values from -0.078125 to 0.078125
- key_weight: bfloat16 [6144, 3072], P('dp', 'mp'), may hold values from -0.078125 to 0.078125
- query_gain: float32 [128], replicated, may hold values from 0.1 to 1.9
- key_gain: float32 [128], replicated, may hold values from 0.1 to 1.9
- cotangent: bfloat16 [12288, 3072], P('dp', 'mp'), may hold values from -0.0625 to 0.0625
Outputs:
- attended: bfloat16 [12288, 3072], P('dp', 'mp')
- embed_grad: float32 [588, 4, 1536], P(None, 'mp', 'dp')
Inputs may be any that keep to these rules, and one draw needn't show every extreme that they name: `patch_counts`: each draw has 4 images of 48 patches in one pack. `pack_index`: the pack of an image held by loader l is l plus one of 0 to 3, modulo the length of the dp axis; the images of one loader go to different packs.
All inputs are finite; a program needn't handle non-finite values.
Results may differ from a plain program's by a relative error of at most 0.015.
Values may be sent and summed in bfloat16 or wider, within the bound.
No kernel may reach another device: no remote copies, remote signals or barrier semaphores. Data moves between devices by JAX's collectives and lax.ppermute only.
A program may use at most 128 MiB of HBM per device.

v0:
```python
import functools

import jax
import jax.numpy as jnp
from jax import lax
from jax.experimental import pallas as pl
from jax.experimental.pallas import tpu as pltpu
from jax.sharding import Mesh
from jax.sharding import PartitionSpec as P

D = 6144
HEADS = 24
HD = 128
PATCH = 588
MOST = 48
IMG_LOAD = 3
REACH = 4
EPS = 1e-06

NY, NZ, NC, NX = 4, 8, 2, 4
NDP = NY * NZ * NC
FX = D // NX
FB = FX // NC
HC = HEADS // NX // NC
HW = HC * HD
ROWS = NC * IMG_LOAD * MOST
EROWS = ROWS + 16
STRIP = FB // NZ
PACK = REACH * MOST
PIECE = FX // NDP
YROWS = NZ * PIECE
NT = (((1,), (1,)), ((), ()))
TN = (((0,), (0,)), ((), ()))
F32 = jnp.float32
BF16 = jnp.bfloat16
HIGH = lax.Precision.HIGHEST


def dot(a, b, dims=(((1,), (0,)), ((), ()))):
    return lax.dot_general(a, b, dims, preferred_element_type=F32)


def ring(v, axis, n, k):
    return lax.ppermute(v, axis, [(i, (i + k) % n) for i in range(n)])


def core_swap(v):
    return ring(v, "core", NC, 1)


def z_shift(v, k):
    return ring(v, "z", NZ, k)


def z_swap(v, step):
    return lax.ppermute(v, "z", [(i, i ^ step) for i in range(NZ)])


def y_shift(v, k):
    return ring(v, "y", NY, k)


def x_shift(v, k):
    return ring(v, "x", NX, k)


def chip_shift(v, k):
    return ring(v, ("y", "z"), NY * NZ, k)


def by_core(core, mine, other, axis):
    return jnp.where(
        core == 0,
        jnp.concatenate([mine, other], axis=axis),
        jnp.concatenate([other, mine], axis=axis),
    )


def turn(pieces, start, axis):
    n = len(pieces)
    double = jnp.concatenate(list(pieces) + list(pieces), axis=axis)
    size = pieces[0].shape[axis]
    return lax.dynamic_slice_in_dim(double, start * size, n * size, axis=axis)


def vmem(n):
    return [pl.BlockSpec(memory_space=pltpu.VMEM)] * n


def regroup(rows):
    wide = rows.astype(F32)
    order = [wide[(2 * q + k) * PIECE : (2 * q + k + 1) * PIECE] for k in range(2) for q in range(2)]
    return jnp.concatenate(order, axis=0).astype(BF16)


def prep_kernel(
    place, counts, packs, wq_in, wk_in, cot_in, pix_in, send, kept, source, wq, wk, cot, pix, sems
):
    y, z, c = place[1], place[2], place[3]
    pairs = ((pix_in, pix), (wq_in, wq), (wk_in, wk), (cot_in, cot))
    copies = [pltpu.make_async_copy(a, b, sems.at[k]) for k, (a, b) in enumerate(pairs)]
    for copy in copies:
        copy.start()
    for copy in copies:
        copy.wait()
    d = (y * NZ + z) * NC + c
    lane = lax.broadcasted_iota(jnp.int32, (MOST, 2 * HW), 1)
    row = lax.broadcasted_iota(jnp.int32, (MOST, 2 * HW), 0)
    source[...] = jnp.zeros_like(source)
    source[:, :PATCH] = pix[...]
    for i in range(IMG_LOAD):
        rows = pl.ds(i * MOST, MOST)
        n = counts[i]
        slot = lax.rem(packs[i] - d + NDP, NDP)
        values = jnp.where(row < n, source[rows, :].astype(F32), 0.0)
        values = jnp.where(lane == PATCH, n.astype(F32), values)
        values = jnp.where(lane == PATCH + 1, slot.astype(F32), values)
        source[rows, :] = values.astype(BF16)

    n_w = 2 * NC * PIECE
    halves = (slice(0, HW), slice(HW, 2 * HW))
    for core in range(NC):

        @pl.when(c == core)
        def _(core=core):
            for k, w in enumerate((wq, wk)):
                kept[k * n_w : (k + 1) * n_w, :] = regroup(w[:, halves[core]])
                send[k * n_w : (k + 1) * n_w, :] = regroup(w[:, halves[1 - core]])
            kept[2 * n_w :, :] = cot[:, halves[core]]
            send[2 * n_w : 2 * n_w + PACK, :] = cot[:, halves[1 - core]]

    at = 2 * n_w + PACK
    for k in range(2):
        send[at + k * IMG_LOAD * MOST : at + (k + 1) * IMG_LOAD * MOST, :] = source[:, halves[k]]


def prep(place, counts, packs, wq, wk, cot, pix):
    n_w = 2 * NC * PIECE
    return pl.pallas_call(
        prep_kernel,
        out_shape=(
            jax.ShapeDtypeStruct((2 * n_w + PACK + 2 * IMG_LOAD * MOST, HW), BF16),
            jax.ShapeDtypeStruct((2 * n_w + PACK, HW), BF16),
            jax.ShapeDtypeStruct((IMG_LOAD * MOST, 2 * HW), BF16),
        ),
        in_specs=[pl.BlockSpec(memory_space=pltpu.SMEM)] * 3
        + [pl.BlockSpec(memory_space=pltpu.HBM)] * 4,
        out_specs=tuple(vmem(3)),
        scratch_shapes=[
            pltpu.VMEM(wq.shape, BF16),
            pltpu.VMEM(wk.shape, BF16),
            pltpu.VMEM(cot.shape, BF16),
            pltpu.VMEM(pix.shape, BF16),
            pltpu.SemaphoreType.DMA((4,)),
        ],
        compiler_params=pltpu.CompilerParams(vmem_limit_bytes=60 * 2**20),
        cost_estimate=pl.CostEstimate(flops=1000000, bytes_accessed=2000000, transcendentals=0),
        name="prep",
    )(place, counts, packs, wq, wk, cot, pix)


def order_kernel(place, *refs):
    pieces, out = refs[:-1], refs[-1]
    for k, piece in enumerate(pieces):
        out[pl.ds(2 * lax.rem(place[1] + k, NY), 2)] = piece[...]


def in_order(place, pieces):
    return pl.pallas_call(
        order_kernel,
        out_shape=jax.ShapeDtypeStruct((NY * NC, STRIP, HW), BF16),
        in_specs=[pl.BlockSpec(memory_space=pltpu.SMEM)] + vmem(len(pieces)),
        out_specs=pl.BlockSpec(memory_space=pltpu.VMEM),
        cost_estimate=pl.CostEstimate(flops=0, bytes_accessed=2000000, transcendentals=0),
        name="order",
    )(place, *pieces)


def embed_kernel(place, source, got, w0, w1, w2, w3, gain, out, pix, facts, weights):
    y, c = place[1], place[3]
    for k, piece in enumerate((w0, w1, w2, w3)):
        at = pl.multiple_of(lax.rem(y + k, NY) * YROWS, YROWS)
        weights[pl.ds(at, YROWS), :] = piece[...]
    half = IMG_LOAD * MOST
    at = 4 * NC * PIECE + PACK
    mine = source[...]
    other = jnp.concatenate([got[at : at + half, :], got[at + half : at + 2 * half, :]], axis=1)
    low = jnp.where(c == 0, mine, other)
    high = jnp.where(c == 0, other, mine)
    pix[:half, :] = low[:, :PATCH]
    pix[half:, :] = high[:, :PATCH]
    first = PATCH // 128 * 128
    for core, part in enumerate((low, high)):
        wide = part[:, first : first + 128].astype(F32)
        for i in range(IMG_LOAD):
            k = core * IMG_LOAD + i
            facts[k : k + 1, :] = wide[i * MOST : i * MOST + 1, :].astype(jnp.int32)
    facts[NC * IMG_LOAD :, :] = jnp.zeros((8 - NC * IMG_LOAD, 128), jnp.int32)
    out[:ROWS, :] = dot(pix[...], weights[...], NT).astype(BF16)
    full = gain[...]
    high = full.astype(BF16)
    rest = full - high.astype(F32)
    mid = rest.astype(BF16)
    low = (rest - mid.astype(F32)).astype(BF16)
    row = lax.broadcasted_iota(jnp.int32, (16, FB), 0)
    out[ROWS:, :] = jnp.where(
        row == 0,
        high.astype(F32),
        jnp.where(row == 1, mid.astype(F32), jnp.where(row == 2, low.astype(F32), 0.0)),
    ).astype(BF16)


def embed(place, source, got, pieces, gain):
    return pl.pallas_call(
        embed_kernel,
        out_shape=(
            jax.ShapeDtypeStruct((EROWS, FB), BF16),
            jax.ShapeDtypeStruct((ROWS, PATCH), BF16),
            jax.ShapeDtypeStruct((8, 128), jnp.int32),
        ),
        in_specs=[pl.BlockSpec(memory_space=pltpu.SMEM)] + vmem(7),
        out_specs=tuple(vmem(3)),
        scratch_shapes=[pltpu.VMEM((FB, PATCH), BF16)],
        compiler_params=pltpu.CompilerParams(vmem_limit_bytes=24 * 2**20),
        cost_estimate=pl.CostEstimate(
            flops=2 * ROWS * FB * PATCH, bytes_accessed=2000000, transcendentals=0
        ),
        name="embed",
    )(place, source, got, *pieces, gain)


def gain_of(rows):
    wide = rows.astype(F32)
    return wide[0:1] + wide[1:2] + wide[2:3]


def head_norm(values):
    center = jnp.mean(values, axis=1, keepdims=True)
    spread = jnp.mean(values * values, axis=1, keepdims=True) - center * center
    inv = lax.rsqrt(spread + EPS)
    return (values - center) * inv, inv


def head_back(grad_hat, unit, inv, gain):
    t = grad_hat * gain
    mean_t = jnp.mean(t, axis=1, keepdims=True)
    second = jnp.mean(t * unit, axis=1, keepdims=True)
    return inv * (t - mean_t - unit * second)


def lanes_sum(v):
    total = v[:, :128]
    for k in range(1, v.shape[1] // 128):
        total = total + v[:, k * 128 : (k + 1) * 128]
    return total


def layer_kernel(*refs):
    place, facts, e_in = refs[:3]
    a_refs, b_refs = refs[3:8], refs[8:17]
    pick, packs, near, far, q_gain, k_gain = refs[17:23]
    att_here, att_near, att_far, own_out, other_out, ms = refs[23:29]
    w, acc, grad, grad_v, acc1, acc2, cot, att, e, normed, values, sems, e_sems = refs[29:]
    x, y, z, c = place[0], place[1], place[2], place[3]
    first = pl.ds(0, HW)
    second = pl.ds(HW, HW)
    copies = []

    def fetch(b):
        return pltpu.make_async_copy(e_in.at[b], e.at[b], e_sems.at[b])

    for b in range(8):
        fetch(b).start()

    def go(src, dst):
        copies.append(pltpu.make_async_copy(src, dst, sems.at[len(copies)]))
        copies[-1].start()

    for core in range(NC):
        for k in range(3):
            yk = lax.rem(y + (0, NY - 1, 1)[k], NY)
            go(a_refs[k].at[:, core], w.at[2 * yk + core, :, :, first])
        for k in range(2):
            yk = lax.rem(y + 2, NY)
            go(a_refs[3 + k].at[:, core], w.at[2 * yk + core, pl.ds(4 * k, 4), :, first])
    for k in range(9):
        zk = lax.rem(z + (0, NZ - 1, 1, NZ - 2, 2, NZ - 3, 3, 4, 4)[k], NZ)
        rows = pl.ds(0, 8) if k < 7 else pl.ds(4 * (k - 7), 4)
        go(b_refs[k], w.at[rows, zk, :, second])
    acc[...] = jnp.zeros_like(acc)
    acc1[...] = jnp.zeros_like(acc1)
    acc2[...] = jnp.zeros_like(acc2)

    def sums(b, carry):
        fetch(b).wait()
        wide = e[b, :ROWS, :].astype(F32)
        acc1[...] += lanes_sum(wide)
        acc2[...] += lanes_sum(wide * wide)
        return carry

    lax.fori_loop(0, 8, sums, 0)
    mean = jnp.sum(acc1[...], axis=1, keepdims=True) * (1.0 / D)
    square = jnp.sum(acc2[...], axis=1, keepdims=True) * (1.0 / D)
    scale = lax.rsqrt(square - mean * mean + EPS)
    lane = lax.broadcasted_iota(jnp.int32, (ROWS, 128), 1)
    ms[...] = jnp.where(lane == 0, mean, scale)

    def norm(b, carry):
        wide = e[b, :ROWS, :].astype(F32)
        gain = gain_of(e[b, ROWS:, :])
        normed[b] = ((wide - mean) * scale * gain).astype(BF16)
        return carry

    lax.fori_loop(0, 8, norm, 0)
    picked = dot(normed[2 * x], pick[0]) + dot(normed[2 * x + 1], pick[1])
    values[...] = picked.astype(BF16)
    n_at = PATCH % 128
    counts = [facts[i, n_at] for i in range(NC * IMG_LOAD)]
    slots = [facts[i, n_at + 1] for i in range(NC * IMG_LOAD)]
    by_slot = (
        (packs[0, 0], packs[1, 1], near[1], near[3]),
        (packs[1, 0], near[0], near[2], far[...]),
    )
    for i, slot in enumerate(slots):
        rows = jnp.zeros((MOST, HW), F32)
        for k in range(REACH):
            piece = by_slot[i // IMG_LOAD][k].astype(F32)
            rows = jnp.where(slot == k, piece, rows)
        cot[i * MOST : (i + 1) * MOST, :] = rows.astype(BF16)
    for copy in copies:
        copy.wait()

    def block(b):
        return w[b].reshape(FB, 2 * HW)

    def project(b, carry):
        acc[...] += dot(normed[b], block(b))
        return carry

    lax.fori_loop(0, 8, project, 0)

    inv_root = HD ** (-0.5)
    span = 2 * MOST
    row = lax.broadcasted_iota(jnp.int32, (span, span), 0)
    col = lax.broadcasted_iota(jnp.int32, (span, span), 1)
    qg, kg = q_gain[...], k_gain[...]
    masks = []
    for g in range(ROWS // span):
        n0, n1 = counts[2 * g], counts[2 * g + 1]
        top_r = jnp.where(row < MOST, n0, n1 + MOST)
        top_c = jnp.where(col < MOST, n0, n1 + MOST)
        same = jnp.where(row < MOST, 0, 1) == jnp.where(col < MOST, 0, 1)
        masks.append(((row < top_r) & (col < top_c) & same, row[:, :1] < top_r[:, :1]))
    for h in range(HC):
        cols = slice(h * HD, (h + 1) * HD)
        kcols = slice(HW + h * HD, HW + (h + 1) * HD)
        q_unit, q_inv = head_norm(acc[:, cols])
        k_unit, k_inv = head_norm(acc[:, kcols])
        q_hat = (q_unit * qg).astype(BF16)
        k_hat = (k_unit * kg).astype(BF16)
        gq, gk = [], []
        for g in range(ROWS // span):
            rows = slice(g * span, (g + 1) * span)
            allowed, live = masks[g]
            q, k, v, go = q_hat[rows], k_hat[rows], values[rows, cols], cot[rows, cols]
            scores = dot(q, k, NT) * inv_root
            raised = jnp.where(allowed, jnp.exp(scores), 0.0)
            totals = jnp.sum(raised, axis=1, keepdims=True)
            totals = jnp.where(live, totals, 1.0)
            probs = raised / totals
            low = probs.astype(BF16)
            att[rows, cols] = dot(low, v).astype(BF16)
            g_probs = dot(go, v, NT)
            grad_v[rows, cols] = dot(low, go, TN).astype(BF16)
            g_scores = probs * (g_probs - jnp.sum(probs * g_probs, axis=1, keepdims=True))
            g_low = (g_scores * inv_root).astype(BF16)
            gq.append(dot(g_low, k))
            gk.append(dot(g_low, q, TN))
        grad[:, cols] = head_back(jnp.concatenate(gq, axis=0), q_unit, q_inv, qg).astype(BF16)
        grad[:, kcols] = head_back(jnp.concatenate(gk, axis=0), k_unit, k_inv, kg).astype(BF16)

    goes = (
        ((att_here, 0), (att_here, 1), (att_near, 0), (att_near, 1)),
        ((att_here, 2), (att_near, 2), (att_near, 3), (att_far, 0)),
    )
    for core in range(NC):
        for k, (out, at) in enumerate(goes[core]):
            rows = jnp.zeros((MOST, HW), F32)
            for i in range(core * IMG_LOAD, (core + 1) * IMG_LOAD):
                piece = att[i * MOST : (i + 1) * MOST, :].astype(F32)
                rows = jnp.where(slots[i] == k, piece, rows)
            out[at] = rows.astype(BF16)

    acc1[...] = jnp.zeros_like(acc1)
    acc2[...] = jnp.zeros_like(acc2)
    mean, scale = ms[:, 0:1], ms[:, 1:2]

    def back(k, core, out, with_values):
        b = 2 * lax.rem(x + k, NX) + core
        part = dot(grad[...], block(b), NT)
        if with_values:
            part = part + dot(grad_v[...], pick[core], NT)
        out[k, :ROWS, :] = part.astype(BF16)
        t = part * gain_of(e[b, ROWS:, :])
        unit = (e[b, :ROWS, :].astype(F32) - mean) * scale
        acc1[...] += lanes_sum(t)
        acc2[...] += lanes_sum(t * unit)

    for out, core in ((other_out, 1 - c), (own_out, c)):
        back(0, core, out, True)

        def step(k, carry, core=core, out=out):
            back(k, core, out, False)
            return carry

        lax.fori_loop(1, NX, step, 0)
    ones = jnp.ones((8, 128), F32)
    stats = []
    for part in (acc1, acc2):
        total = lax.dot_general(ones, part[...], NT, preferred_element_type=F32, precision=HIGH)
        stats.append(jnp.concatenate([total, jnp.zeros((8, FB - ROWS), F32)], axis=1))
    rows = stat_rows(stats[0][:1], stats[1][:1])
    for out in (own_out, other_out):
        for k in range(NX):
            out[k, ROWS:, :] = rows


def stat_rows(first, second):
    row = lax.broadcasted_iota(jnp.int32, (16, FB), 0)
    parts = []
    for v in (first, second):
        high = v.astype(BF16).astype(F32)
        parts += [high, v - high]
    out = jnp.zeros((16, FB), F32)
    for k in range(4):
        out = jnp.where(row == k, parts[k], out)
    return out.astype(BF16)


def stats_of(rows):
    wide = rows.astype(F32)
    return wide[0:1] + wide[1:2], wide[2:3] + wide[3:4]


def layer(place, facts, blocks, a_pieces, b_pieces, pick, cot_pieces, q_gain, k_gain):
    hbm = [pl.BlockSpec(memory_space=pltpu.HBM)]
    smem = [pl.BlockSpec(memory_space=pltpu.SMEM)]
    flops = 4 * ROWS * D * 2 * HW
    return pl.pallas_call(
        layer_kernel,
        out_shape=(
            jax.ShapeDtypeStruct((3, MOST, HW), BF16),
            jax.ShapeDtypeStruct((4, MOST, HW), BF16),
            jax.ShapeDtypeStruct((1, MOST, HW), BF16),
            jax.ShapeDtypeStruct((NX, EROWS, FB), BF16),
            jax.ShapeDtypeStruct((NX, EROWS, FB), BF16),
            jax.ShapeDtypeStruct((ROWS, 128), F32),
        ),
        in_specs=smem * 2 + hbm * 15 + vmem(6),
        out_specs=tuple(vmem(6)),
        scratch_shapes=[
            pltpu.VMEM((8, NZ, STRIP, 2 * HW), BF16),
            pltpu.VMEM((ROWS, 2 * HW), F32),
            pltpu.VMEM((ROWS, 2 * HW), BF16),
            pltpu.VMEM((ROWS, HW), BF16),
            pltpu.VMEM((ROWS, 128), F32),
            pltpu.VMEM((ROWS, 128), F32),
            pltpu.VMEM((ROWS, HW), BF16),
            pltpu.VMEM((ROWS, HW), BF16),
            pltpu.VMEM((8, EROWS, FB), BF16),
            pltpu.VMEM((8, ROWS, FB), BF16),
            pltpu.VMEM((ROWS, HW), BF16),
            pltpu.SemaphoreType.DMA((19,)),
            pltpu.SemaphoreType.DMA((8,)),
        ],
        compiler_params=pltpu.CompilerParams(vmem_limit_bytes=60 * 2**20),
        cost_estimate=pl.CostEstimate(flops=flops, bytes_accessed=20000000, transcendentals=100000),
        name="layer",
    )(place, facts, blocks, *a_pieces, *b_pieces, pick, *cot_pieces, q_gain, k_gain)


def pair_kernel(own, got, *outs):
    for k, out in enumerate(outs):
        out[:ROWS, :] = (own[k, :ROWS, :].astype(F32) + got[k, :ROWS, :].astype(F32)).astype(BF16)
        a, b = stats_of(own[k, ROWS:, :]), stats_of(got[k, ROWS:, :])
        out[ROWS:, :] = stat_rows(a[0] + b[0], a[1] + b[1])


def pair_sum(own, got):
    return pl.pallas_call(
        pair_kernel,
        out_shape=(jax.ShapeDtypeStruct((EROWS, FB), BF16),) * NX,
        in_specs=vmem(2),
        out_specs=tuple(vmem(NX)),
        compiler_params=pltpu.CompilerParams(vmem_limit_bytes=16 * 2**20),
        cost_estimate=pl.CostEstimate(flops=1000000, bytes_accessed=6000000, transcendentals=0),
        name="pair_sum",
    )(own, got)


def embed_back_kernel(
    place, own, r1, r2, r3, e_own, ms, pix, own_out, send_out, full
):
    y = place[1]
    part = own[:ROWS, :].astype(F32)
    sums = stats_of(own[ROWS:, :])
    for ref in (r1, r2, r3):
        part = part + ref[:ROWS, :].astype(F32)
        more = stats_of(ref[ROWS:, :])
        sums = (sums[0] + more[0], sums[1] + more[1])
    mean, scale = ms[:, 0:1], ms[:, 1:2]
    gain = gain_of(e_own[ROWS:, :])
    chooser = jnp.where(lax.broadcasted_iota(jnp.int32, (8, 128), 0) == 0, 1.0 / D, 0.0)
    columns = []
    for v in sums:
        tall = jnp.broadcast_to(v[:, :ROWS], (8, ROWS))
        columns.append(
            lax.dot_general(tall, chooser, TN, preferred_element_type=F32, precision=HIGH)[:, :1]
        )
    t = part * gain
    unit = (e_own[:ROWS, :].astype(F32) - mean) * scale
    grad = (scale * (t - columns[0] - unit * columns[1])).astype(BF16)
    full[...] = dot(grad, pix[...], TN)
    for k in range(NY):
        at = pl.multiple_of(lax.rem(y + k, NY) * YROWS, YROWS)
        piece = full[pl.ds(at, YROWS), :]
        if k == 0:
            own_out[...] = piece
        else:
            send_out[k - 1] = piece.astype(BF16)


def embed_back(place, *args):
    return pl.pallas_call(
        embed_back_kernel,
        out_shape=(
            jax.ShapeDtypeStruct((YROWS, PATCH), F32),
            jax.ShapeDtypeStruct((NY - 1, YROWS, PATCH), BF16),
        ),
        in_specs=[pl.BlockSpec(memory_space=pltpu.SMEM)] + vmem(7),
        out_specs=tuple(vmem(2)),
        scratch_shapes=[pltpu.VMEM((FB, PATCH), F32)],
        compiler_params=pltpu.CompilerParams(vmem_limit_bytes=32 * 2**20),
        cost_estimate=pl.CostEstimate(
            flops=2 * ROWS * FB * PATCH, bytes_accessed=5000000, transcendentals=0
        ),
        name="embed_back",
    )(place, *args)


def per_device(
    pixels,
    patch_counts,
    pack_index,
    embed_weight,
    norm_gain,
    query_weight,
    key_weight,
    query_gain,
    key_gain,
    cotangent,
):
    x, y, z, c = [lax.axis_index(name) for name in ("x", "y", "z", "core")]
    d = (y * NZ + z) * NC + c
    place = jnp.stack([x, y, z, c]).astype(jnp.int32)

    strip = jnp.swapaxes(embed_weight.reshape(PATCH, PIECE), 0, 1)
    strip = by_core(z % 2, strip, z_swap(strip, 1), 0)
    sent, kept, source = prep(
        place, patch_counts, pack_index, query_weight, key_weight, cotangent, pixels
    )
    got = core_swap(sent)
    n_w = 2 * NC * PIECE
    shards = []
    for k in range(2):
        rows = slice(k * n_w, (k + 1) * n_w)
        mine = kept[rows].reshape(NC, 2 * PIECE, HW)
        shards.append(by_core(c, mine, got[rows].reshape(NC, 2 * PIECE, HW), 1))
    a0, b0 = shards

    after = lax.optimization_barrier
    a_own = lax.all_gather(a0, "z", axis=0, tiled=False)
    b_near = [y_shift(b0, -k) for k in range(1, NY)]
    for step in (2, 4):
        strip = by_core(z // step % 2, strip, z_swap(strip, step), 0)
    strip, b_near = after((strip, b_near))
    b_own = in_order(place, [b0] + b_near)
    embed_pieces = [strip] + [y_shift(strip, -k) for k in range(1, NY)]
    bl1, br1 = z_shift(b_own, 1), z_shift(b_own, -1)
    bl2, br2 = z_shift(bl1, 1), z_shift(br1, -1)
    bl3, br3 = z_shift(bl2, 1), z_shift(br2, -1)
    bl4, br4 = z_shift(bl3[:4], 1), z_shift(br3[4:], -1)
    a_low, a_high = y_shift(a_own, 1), y_shift(a_own, -1)
    a_pieces = [a_own, a_low, a_high, y_shift(a_low[:4], 1), y_shift(a_high[4:], -1)]
    b_pieces = [b_own, bl1, br1, bl2, br2, bl3, br3, bl4, br4]

    gain_here = jnp.where(
        c == 0, norm_gain.reshape(-1, NC, PIECE)[:, 0], norm_gain.reshape(-1, NC, PIECE)[:, 1]
    ).reshape(1, FB)
    e_own, pix, facts = embed(place, source, got, embed_pieces, gain_here)
    blocks = lax.all_gather(e_own, ("x", "core"), axis=0, tiled=False)

    kept_cot, got_cot, bl2 = after((kept[2 * n_w :], got[2 * n_w : 2 * n_w + PACK], bl2))
    packs = by_core(c, kept_cot[None], got_cot[None], 0)
    packs = packs.reshape(NC, REACH, MOST, HW)
    near = chip_shift(jnp.stack([packs[0, 1], packs[0, 2], packs[1, 2], packs[1, 3]]), -1)
    far = chip_shift(packs[0, 3], -2)

    column = jnp.arange(HW, dtype=jnp.int32)[None, None, :]
    feature = (c * HC + column // HD) * (D // HEADS) + column % HD
    at = (feature // (NC * PIECE)) * PIECE + feature % PIECE
    part = (feature // PIECE) % NC
    pick = (
        (jnp.arange(FB, dtype=jnp.int32)[None, :, None] == at)
        & (jnp.arange(NC, dtype=jnp.int32)[:, None, None] == part)
    ).astype(BF16)

    att_here, att_near, att_far, own_grad, other_grad, ms = layer(
        place,
        facts,
        blocks,
        a_pieces,
        b_pieces,
        pick,
        (packs, near, far),
        query_gain.reshape(1, HD),
        key_gain.reshape(1, HD),
    )

    pair = pair_sum(own_grad, core_swap(other_grad))
    arrived = [x_shift(pair[k], k) for k in range(1, NX)]
    grad_own, grad_send = embed_back(place, pair[0], *arrived, e_own, ms, pix)
    total = grad_own
    for k in range(1, NY):
        total = total + y_shift(grad_send[k - 1], k).astype(F32)
    total = total.reshape(NZ, PIECE, PATCH)
    sent = total.astype(BF16)
    arrived = lax.all_to_all(sent, "z", 0, 0)
    embed_grad = jnp.sum(arrived.astype(F32), axis=0)
    embed_grad = jnp.swapaxes(embed_grad, 0, 1).reshape(PATCH, 1, PIECE)

    near = chip_shift(att_near, 1)
    far = chip_shift(att_far, 2)
    packs = jnp.concatenate(
        [att_here[0], near[2], near[0], far[0], att_here[2], att_here[1], near[3], near[1]], axis=0
    ).reshape(NC, PACK, HW)
    keep = jnp.where(c == 0, packs[0], packs[1])
    give = jnp.where(c == 0, packs[1], packs[0])
    attended = by_core(c, keep, core_swap(give), 1)
    return attended, embed_grad


def solution(mesh):
    chips = Mesh(mesh.devices.reshape(NY, NZ, NC, NX), ("y", "z", "core", "x"))
    dp = ("y", "z", "core")
    placed = (
        P(dp, None),
        P(dp),
        P(dp),
        P(None, "x", dp),
        P("x"),
        P(dp, "x"),
        P(dp, "x"),
        P(),
        P(),
        P(dp, "x"),
    )
    return jax.shard_map(
        per_device,
        mesh=chips,
        in_specs=placed,
        out_specs=(P(dp, "x"), P(None, "x", dp)),
        check_vma=False,
    )
```

profile of v0, /device:TPU:32, one launch (start us, length us, event | category | flops | bytes accessed | tf_op | source)
XLA Modules:
  0.0 208.4 jit_solution(14160460440023099211)
XLA Ops:
  7.9 3.0 %prep.1 = (bf16[672,384]{1,0:T(8,128)(2,1)}, bf16[384,384]{1,0:T(8,128)(2,1)}, bf16[144,768]{1,0:T(8,128)(2,1)}) custom-call(s32[4]{0:T(128)} %pad_add_fusion.place.refs_0_, s32[3]{0:T(128)} %counts.1, s32[3]{0:T(128)} %packs.1, bf16[96,768]{1,0:T(8,128)(2,1)} %wq_in.1, bf16[96,768]{1,0:T(8,128)(2,1)} %wk_in.1, bf16[192,768]{1,0:T(8,128)(2,1)} %cot_in.1, ...), custom_call_target="tpu_custom_call" | custom-call | flops 1000000 | bytes 2000000 | tf_op jit(solution)/shard_map/prep/pallas_call | solution.py:139
  15.8 2.0 collective-permute-done.1
  17.9 3.4 %collective-permute-start.2 = (bf16[48,588]{1,0:T(8,128)(2,1)S(1)}, bf16[48,588]{1,0:T(8,128)(2,1)S(1)}, u32[]{:S(2)}, u32[]{:S(2)}) collective-permute-start(bf16[48,588]{1,0:T(8,128)(2,1)S(1)} %maximum_select_fusion.6), channel_id=1, source_target_pairs={{0,16},{8,24},{16,0},{24,8},{32,48},{40,56},{48,32},{56,40},{1,17}... | collective-permute-start | bytes 169352 | tf_op jit(solution)/shard_map/ppermute | solution.py:56
  21.3 2.3 %collective-permute-done.2 = bf16[48,588]{1,0:T(8,128)(2,1)S(1)} collective-permute-done((bf16[48,588]{1,0:T(8,128)(2,1)S(1)}, bf16[48,588]{1,0:T(8,128)(2,1)S(1)}, u32[]{:S(2)}, u32[]{:S(2)}) %collective-permute-start.2) | collective-permute-done | bytes 56480 | tf_op jit(solution)/shard_map/ppermute | solution.py:56
  23.6 6.1 %collective-permute-start.3 = (bf16[96,588]{1,0:T(8,128)(2,1)S(1)}, bf16[96,588]{1,0:T(8,128)(2,1)S(1)}, u32[]{:S(2)}, u32[]{:S(2)}) collective-permute-start(bf16[96,588]{1,0:T(8,128)(2,1)S(1)} %maximum_select_fusion.5), channel_id=1, source_target_pairs={{0,32},{8,40},{16,48},{24,56},{32,0},{40,8},{48,16},{56,24},{1,33}... | collective-permute-start | bytes 338696 | tf_op jit(solution)/shard_map/ppermute | solution.py:56
  31.3 2.9 %collective-permute-start.5 = (bf16[2,96,384]{2,1,0:T(8,128)(2,1)S(1)}, bf16[2,96,384]{2,1,0:T(8,128)(2,1)S(1)}, u32[]{:S(2)}, u32[]{:S(2)}) collective-permute-start(bf16[2,96,384]{2,1,0:T(8,128)(2,1)S(1)} %maximum_select_fusion.3.refs_0_), channel_id=1, source_target_pairs={{0,128},{64,192},{128,0},{192,64},{1,129},{65,193},{129,1},{193,65... | collective-permute-start | bytes 442376 | tf_op jit(solution)/shard_map/ppermute | solution.py:44
  40.6 2.8 %collective-permute-start.8 = (bf16[192,588]{1,0:T(8,128)(2,1)S(1)}, bf16[192,588]{1,0:T(8,128)(2,1)S(1)}, u32[]{:S(2)}, u32[]{:S(2)}) collective-permute-start(bf16[192,588]{1,0:T(8,128)(2,1)S(1)} %maximum_select_fusion.2.w0), channel_id=1, source_target_pairs={{0,128},{64,192},{128,0},{192,64},{1,129},{65,193},{129,1},{193,65... | collective-permute-start | bytes 677384 | tf_op jit(solution)/shard_map/ppermute | solution.py:44
  44.7 3.0 %collective-permute-done.9.w3 = bf16[192,588]{1,0:T(8,128)(2,1)S(1)} collective-permute-done((bf16[192,588]{1,0:T(8,128)(2,1)S(1)}, bf16[192,588]{1,0:T(8,128)(2,1)S(1)}, u32[]{:S(2)}, u32[]{:S(2)}) %collective-permute-start.9) | collective-permute-done | bytes 225824 | tf_op jit(solution)/shard_map/ppermute | solution.py:44
  47.7 2.6 %collective-permute-done.8.w2 = bf16[192,588]{1,0:T(8,128)(2,1)S(1)} collective-permute-done((bf16[192,588]{1,0:T(8,128)(2,1)S(1)}, bf16[192,588]{1,0:T(8,128)(2,1)S(1)}, u32[]{:S(2)}, u32[]{:S(2)}) %collective-permute-start.8) | collective-permute-done | bytes 225824 | tf_op jit(solution)/shard_map/ppermute | solution.py:44
  50.5 2.0 embed.1
  53.2 2.0 order.1.refs_8_
  57.3 2.7 %collective-permute-start.11 = (bf16[8,2,96,384]{3,2,1,0:T(8,128)(2,1)}, bf16[8,2,96,384]{3,2,1,0:T(8,128)(2,1)S(1)}, u32[]{:S(2)}, u32[]{:S(2)}) collective-permute-start(bf16[8,2,96,384]{3,2,1,0:T(8,128)(2,1)} %all-gather.4.cloned.1.call-done.refs_3_), channel_id=1, source_target_pairs={{0,192},{64,0},{128,64},{192,128},{1,193},{65,1},{129,65},{193,129... | collective-permute-start | bytes 3538952 | tf_op jit(solution)/shard_map/ppermute | solution.py:44
  59.9 8.8 %collective-permute-done.15.refs_10_ = bf16[8,96,384]{2,1,0:T(8,128)(2,1)} collective-permute-done((bf16[8,96,384]{2,1,0:T(8,128)(2,1)}, bf16[8,96,384]{2,1,0:T(8,128)(2,1)}, u32[]{:S(2)}, u32[]{:S(2)}) %collective-permute-start.15) | collective-permute-done | bytes 589856 | tf_op jit(solution)/shard_map/ppermute | solution.py:44
  70.9 9.6 %collective-permute-done.17.refs_12_ = bf16[8,96,384]{2,1,0:T(8,128)(2,1)} collective-permute-done((bf16[8,96,384]{2,1,0:T(8,128)(2,1)}, bf16[8,96,384]{2,1,0:T(8,128)(2,1)}, u32[]{:S(2)}, u32[]{:S(2)}) %collective-permute-start.17) | collective-permute-done | bytes 589856 | tf_op jit(solution)/shard_map/ppermute | solution.py:44
  80.5 3.7 %collective-permute-start.19 = (bf16[8,96,384]{2,1,0:T(8,128)(2,1)}, bf16[8,96,384]{2,1,0:T(8,128)(2,1)S(1)}, u32[]{:S(2)}, u32[]{:S(2)}) collective-permute-start(bf16[8,96,384]{2,1,0:T(8,128)(2,1)} %collective-permute-done.17.refs_12_), channel_id=1, source_target_pairs={{0,56},{8,0},{16,8},{24,16},{32,24},{40,32},{48,40},{56,48},{1,57}... | collective-permute-start | bytes 1769480 | tf_op jit(solution)/shard_map/ppermute | solution.py:44
  86.0 4.5 %collective-permute-start.13 = (bf16[4,2,96,384]{3,2,1,0:T(8,128)(2,1)S(1)}, bf16[4,2,96,384]{3,2,1,0:T(8,128)(2,1)S(1)}, u32[]{:S(2)}, u32[]{:S(2)}) collective-permute-start(bf16[4,2,96,384]{3,2,1,0:T(8,128)(2,1)S(1)} %slice.121), channel_id=1, source_target_pairs={{0,192},{64,0},{128,64},{192,128},{1,193},{65,1},{129,65},{193,129... | collective-permute-start | bytes 1769480 | tf_op jit(solution)/shard_map/ppermute | solution.py:44
  90.8 8.5 %collective-permute-start.23 = (bf16[48,384]{1,0:T(8,128)(2,1)S(1)}, bf16[48,384]{1,0:T(8,128)(2,1)S(1)}, u32[]{:S(2)}, u32[]{:S(2)}) collective-permute-start(bf16[48,384]{1,0:T(8,128)(2,1)S(1)} %get-tuple-element.57), channel_id=1, source_target_pairs={{0,240},{8,248},{16,0},{24,8},{32,16},{40,24},{48,32},{56,40},{64,... | collective-permute-start | bytes 110600 | tf_op jit(solution)/shard_map/ppermute | solution.py:44
  99.5 2.1 collective-permute-start.20
  105.0 2.8 %collective-permute-done.22.refs_19_ = bf16[4,48,384]{2,1,0:T(8,128)(2,1)S(1)} collective-permute-done((bf16[4,48,384]{2,1,0:T(8,128)(2,1)S(1)}, bf16[4,48,384]{2,1,0:T(8,128)(2,1)S(1)}, u32[]{:S(2)}, u32[]{:S(2)}) %collective-permute-start.22) | collective-permute-done | bytes 147488 | tf_op jit(solution)/shard_map/ppermute | solution.py:44
  108.8 22.8 %layer.1 = (bf16[3,48,384]{2,1,0:T(8,128)(2,1)}, bf16[4,48,384]{2,1,0:T(8,128)(2,1)}, bf16[1,48,384]{2,1,0:T(8,128)(2,1)}, bf16[4,304,768]{2,1,0:T(8,128)(2,1)},...) custom-call(s32[4]{0:T(128)} %pad_add_fusion.place.refs_0_, s32[8,128]{1,0:T(8,128)} %copy-done.5, ...), custom_call_target="tpu_custom_call" | custom-call | flops 5435817984 | bytes 20000000 | tf_op jit(solution)/shard_map/layer/pallas_call | solution.py:449
  131.7 4.0 %collective-permute-done.27.got = bf16[4,304,768]{2,1,0:T(8,128)(2,1)S(1)} collective-permute-done((bf16[4,304,768]{2,1,0:T(8,128)(2,1)}, bf16[4,304,768]{2,1,0:T(8,128)(2,1)S(1)}, u32[]{:S(2)}, u32[]{:S(2)}) %collective-permute-start.27) | collective-permute-done | bytes 1867808 | tf_op jit(solution)/shard_map/ppermute | solution.py:44
  139.2 2.6 %collective-permute-start.29 = (bf16[304,768]{1,0:T(8,128)(2,1)S(1)}, bf16[304,768]{1,0:T(8,128)(2,1)S(1)}, u32[]{:S(2)}, u32[]{:S(2)}) collective-permute-start(bf16[304,768]{1,0:T(8,128)(2,1)S(1)} %get-tuple-element.44), channel_id=1, source_target_pairs={{0,2},{1,3},{2,0},{3,1},{4,6},{5,7},{6,4},{7,5},{8,10},{9,11},{10,... | collective-permute-start | bytes 1400840 | tf_op jit(solution)/shard_map/ppermute | solution.py:44
  143.3 2.6 %collective-permute-start.25 = (bf16[1,48,384]{2,1,0:T(8,128)(2,1)S(1)}, bf16[1,48,384]{2,1,0:T(8,128)(2,1)S(1)}, u32[]{:S(2)}, u32[]{:S(2)}) collective-permute-start(bf16[1,48,384]{2,1,0:T(8,128)(2,1)S(1)} %copy-done.23), channel_id=1, source_target_pairs={{0,16},{8,24},{16,32},{24,40},{32,48},{40,56},{48,64},{56,72},{64,... | collective-permute-start | bytes 110600 | tf_op jit(solution)/shard_map/ppermute | solution.py:44
  146.9 4.8 %collective-permute-done.28.r1 = bf16[304,768]{1,0:T(8,128)(2,1)S(1)} collective-permute-done((bf16[304,768]{1,0:T(8,128)(2,1)S(1)}, bf16[304,768]{1,0:T(8,128)(2,1)S(1)}, u32[]{:S(2)}, u32[]{:S(2)}) %collective-permute-start.28) | collective-permute-done | bytes 466976 | tf_op jit(solution)/shard_map/ppermute | solution.py:44
  151.8 10.8 %collective-permute-done.29.r2 = bf16[304,768]{1,0:T(8,128)(2,1)S(1)} collective-permute-done((bf16[304,768]{1,0:T(8,128)(2,1)S(1)}, bf16[304,768]{1,0:T(8,128)(2,1)S(1)}, u32[]{:S(2)}, u32[]{:S(2)}) %collective-permute-start.29) | collective-permute-done | bytes 466976 | tf_op jit(solution)/shard_map/ppermute | solution.py:44
  162.6 2.9 %embed_back.1 = (f32[192,588]{1,0:T(8,128)S(1)}, bf16[3,192,588]{2,1,0:T(8,128)(2,1)S(1)}) custom-call(s32[4]{0:T(128)S(1)} %copy-done.4, bf16[304,768]{1,0:T(8,128)(2,1)S(1)} %get-tuple-element.42.own, bf16[304,768]{1,0:T(8,128)(2,1)S(1)} %collective-permute-done.28.r1, bf16[304,768]{1,0:T(8,128)(2,1)S(1)} %collective-permute-done.29.r2, ...), custom_call_target="tpu_custom_call" | custom-call | flops 260112384 | bytes 5000000 | tf_op jit(solution)/shard_map/embed_back/pallas_call | solution.py:534
  165.6 4.6 %collective-permute-start.31 = (bf16[192,588]{1,0:T(8,128)(2,1)S(1)}, bf16[192,588]{1,0:T(8,128)(2,1)S(1)}, u32[]{:S(2)}, u32[]{:S(2)}) collective-permute-start(bf16[192,588]{1,0:T(8,128)(2,1)S(1)} %get-tuple-element.50), channel_id=1, source_target_pairs={{0,64},{64,128},{128,192},{192,0},{1,65},{65,129},{129,193},{193,1... | collective-permute-start | bytes 677384 | tf_op jit(solution)/shard_map/ppermute | solution.py:44
  172.3 4.2 %collective-permute-done.31 = bf16[192,588]{1,0:T(8,128)(2,1)S(1)} collective-permute-done((bf16[192,588]{1,0:T(8,128)(2,1)S(1)}, bf16[192,588]{1,0:T(8,128)(2,1)S(1)}, u32[]{:S(2)}, u32[]{:S(2)}) %collective-permute-start.31) | collective-permute-done | bytes 225824 | tf_op jit(solution)/shard_map/ppermute | solution.py:44
  176.6 2.5 %collective-permute-done.33 = bf16[192,588]{1,0:T(8,128)(2,1)S(1)} collective-permute-done((bf16[192,588]{1,0:T(8,128)(2,1)S(1)}, bf16[192,588]{1,0:T(8,128)(2,1)S(1)}, u32[]{:S(2)}, u32[]{:S(2)}) %collective-permute-start.33) | collective-permute-done | bytes 225824 | tf_op jit(solution)/shard_map/ppermute | solution.py:44
  179.1 3.4 %collective-permute-done.32 = bf16[192,588]{1,0:T(8,128)(2,1)S(1)} collective-permute-done((bf16[192,588]{1,0:T(8,128)(2,1)S(1)}, bf16[192,588]{1,0:T(8,128)(2,1)S(1)}, u32[]{:S(2)}, u32[]{:S(2)}) %collective-permute-start.32) | collective-permute-done | bytes 225824 | tf_op jit(solution)/shard_map/ppermute | solution.py:44
  183.3 8.8 %all-to-all-start = ((bf16[8,24,588]{2,1,0:T(8,128)(2,1)}), bf16[8,24,588]{2,1,0:T(8,128)(2,1)S(1)}, u32[]{:S(2)}, u32[]{:S(2)}) async-start(bf16[8,24,588]{2,1,0:T(8,128)(2,1)} %bitcast.32), calls=%async_computation | async-start | bytes 491520 | tf_op jit(solution)/shard_map/all_to_all | solution.py:638
  194.4 6.5 %all-to-all-done = bf16[8,24,588]{2,1,0:T(8,128)(2,1)S(1)} async-done(((bf16[8,24,588]{2,1,0:T(8,128)(2,1)}), bf16[8,24,588]{2,1,0:T(8,128)(2,1)S(1)}, u32[]{:S(2)}, u32[]{:S(2)}) %all-to-all-start) | async-done | bytes 225824 | tf_op jit(solution)/shard_map/all_to_all | solution.py:638
  (131 shorter events, 38.6 us)
Async XLA Ops:
  7.2 50.1 %all-gather.4.cloned.1.call-start = ((), (), s32[]{:S(2)}) async-start(), calls=%async_computation.1 | async-start | bytes 1327104 | tf_op jit(solution)/shard_map/all_gather | solution.py:582
  13.9 94.8 %all-gather.6.cloned.1.call-start = ((), (), s32[]{:S(2)}) async-start(), calls=%async_computation.2 | async-start | bytes 4202496 | tf_op jit(solution)/shard_map/all_gather | solution.py:601
  17.9 5.6 %collective-permute-start.2 = (bf16[48,588]{1,0:T(8,128)(2,1)S(1)}, bf16[48,588]{1,0:T(8,128)(2,1)S(1)}, u32[]{:S(2)}, u32[]{:S(2)}) collective-permute-start(bf16[48,588]{1,0:T(8,128)(2,1)S(1)} %maximum_select_fusion.6), channel_id=1, source_target_pairs={{0,16},{8,24},{16,0},{24,8},{32,48},{40,56},{48,32},{56,40},{1,17}... | collective-permute-start | bytes 169352 | tf_op jit(solution)/shard_map/ppermute | solution.py:56
  23.6 12.2 %collective-permute-start.3 = (bf16[96,588]{1,0:T(8,128)(2,1)S(1)}, bf16[96,588]{1,0:T(8,128)(2,1)S(1)}, u32[]{:S(2)}, u32[]{:S(2)}) collective-permute-start(bf16[96,588]{1,0:T(8,128)(2,1)S(1)} %maximum_select_fusion.5), channel_id=1, source_target_pairs={{0,32},{8,40},{16,48},{24,56},{32,0},{40,8},{48,16},{56,24},{1,33}... | collective-permute-start | bytes 338696 | tf_op jit(solution)/shard_map/ppermute | solution.py:56
  29.7 7.4 %collective-permute-start.6 = (bf16[2,96,384]{2,1,0:T(8,128)(2,1)S(1)}, bf16[2,96,384]{2,1,0:T(8,128)(2,1)S(1)}, u32[]{:S(2)}, u32[]{:S(2)}) collective-permute-start(bf16[2,96,384]{2,1,0:T(8,128)(2,1)S(1)} %maximum_select_fusion.3.refs_0_), channel_id=1, source_target_pairs={{0,64},{64,128},{128,192},{192,0},{1,65},{65,129},{129,193},{193,1... | collective-permute-start | bytes 442376 | tf_op jit(solution)/shard_map/ppermute | solution.py:44
  31.3 7.6 %collective-permute-start.5 = (bf16[2,96,384]{2,1,0:T(8,128)(2,1)S(1)}, bf16[2,96,384]{2,1,0:T(8,128)(2,1)S(1)}, u32[]{:S(2)}, u32[]{:S(2)}) collective-permute-start(bf16[2,96,384]{2,1,0:T(8,128)(2,1)S(1)} %maximum_select_fusion.3.refs_0_), channel_id=1, source_target_pairs={{0,128},{64,192},{128,0},{192,64},{1,129},{65,193},{129,1},{193,65... | collective-permute-start | bytes 442376 | tf_op jit(solution)/shard_map/ppermute | solution.py:44
  39.4 8.3 %collective-permute-start.9 = (bf16[192,588]{1,0:T(8,128)(2,1)S(1)}, bf16[192,588]{1,0:T(8,128)(2,1)S(1)}, u32[]{:S(2)}, u32[]{:S(2)}) collective-permute-start(bf16[192,588]{1,0:T(8,128)(2,1)S(1)} %maximum_select_fusion.2.w0), channel_id=1, source_target_pairs={{0,64},{64,128},{128,192},{192,0},{1,65},{65,129},{129,193},{193,1... | collective-permute-start | bytes 677384 | tf_op jit(solution)/shard_map/ppermute | solution.py:44
  40.6 9.8 %collective-permute-start.8 = (bf16[192,588]{1,0:T(8,128)(2,1)S(1)}, bf16[192,588]{1,0:T(8,128)(2,1)S(1)}, u32[]{:S(2)}, u32[]{:S(2)}) collective-permute-start(bf16[192,588]{1,0:T(8,128)(2,1)S(1)} %maximum_select_fusion.2.w0), channel_id=1, source_target_pairs={{0,128},{64,192},{128,0},{192,64},{1,129},{65,193},{129,1},{193,65... | collective-permute-start | bytes 677384 | tf_op jit(solution)/shard_map/ppermute | solution.py:44
  43.4 7.1 %collective-permute-start.7 = (bf16[192,588]{1,0:T(8,128)(2,1)S(1)}, bf16[192,588]{1,0:T(8,128)(2,1)S(1)}, u32[]{:S(2)}, u32[]{:S(2)}) collective-permute-start(bf16[192,588]{1,0:T(8,128)(2,1)S(1)} %maximum_select_fusion.2.w0), channel_id=1, source_target_pairs={{0,192},{64,0},{128,64},{192,128},{1,193},{65,1},{129,65},{193,129... | collective-permute-start | bytes 677384 | tf_op jit(solution)/shard_map/ppermute | solution.py:44
  55.2 13.5 %collective-permute-start.15 = (bf16[8,96,384]{2,1,0:T(8,128)(2,1)}, bf16[8,96,384]{2,1,0:T(8,128)(2,1)}, u32[]{:S(2)}, u32[]{:S(2)}) collective-permute-start(bf16[8,96,384]{2,1,0:T(8,128)(2,1)} %order.1.refs_8_), channel_id=1, source_target_pairs={{0,56},{8,0},{16,8},{24,16},{32,24},{40,32},{48,40},{56,48},{1,57}... | collective-permute-start | bytes 1769480 | tf_op jit(solution)/shard_map/ppermute | solution.py:44
  57.0 13.9 %collective-permute-start.14 = (bf16[8,96,384]{2,1,0:T(8,128)(2,1)}, bf16[8,96,384]{2,1,0:T(8,128)(2,1)}, u32[]{:S(2)}, u32[]{:S(2)}) collective-permute-start(bf16[8,96,384]{2,1,0:T(8,128)(2,1)} %order.1.refs_8_), channel_id=1, source_target_pairs={{0,8},{8,16},{16,24},{24,32},{32,40},{40,48},{48,56},{56,0},{1,9},... | collective-permute-start | bytes 1769480 | tf_op jit(solution)/shard_map/ppermute | solution.py:44
  57.3 28.7 %collective-permute-start.11 = (bf16[8,2,96,384]{3,2,1,0:T(8,128)(2,1)}, bf16[8,2,96,384]{3,2,1,0:T(8,128)(2,1)S(1)}, u32[]{:S(2)}, u32[]{:S(2)}) collective-permute-start(bf16[8,2,96,384]{3,2,1,0:T(8,128)(2,1)} %all-gather.4.cloned.1.call-done.refs_3_), channel_id=1, source_target_pairs={{0,192},{64,0},{128,64},{192,128},{1,193},{65,1},{129,65},{193,129... | collective-permute-start | bytes 3538952 | tf_op jit(solution)/shard_map/ppermute | solution.py:44
  59.9 30.6 %collective-permute-start.10 = (bf16[8,2,96,384]{3,2,1,0:T(8,128)(2,1)}, bf16[8,2,96,384]{3,2,1,0:T(8,128)(2,1)S(1)}, u32[]{:S(2)}, u32[]{:S(2)}) collective-permute-start(bf16[8,2,96,384]{3,2,1,0:T(8,128)(2,1)} %all-gather.4.cloned.1.call-done.refs_3_), channel_id=1, source_target_pairs={{0,64},{64,128},{128,192},{192,0},{1,65},{65,129},{129,193},{193,1... | collective-permute-start | bytes 3538952 | tf_op jit(solution)/shard_map/ppermute | solution.py:44
  68.7 11.8 %collective-permute-start.17 = (bf16[8,96,384]{2,1,0:T(8,128)(2,1)}, bf16[8,96,384]{2,1,0:T(8,128)(2,1)}, u32[]{:S(2)}, u32[]{:S(2)}) collective-permute-start(bf16[8,96,384]{2,1,0:T(8,128)(2,1)} %collective-permute-done.15.refs_10_), channel_id=1, source_target_pairs={{0,56},{8,0},{16,8},{24,16},{32,24},{40,32},{48,40},{56,48},{1,57}... | collective-permute-start | bytes 1769480 | tf_op jit(solution)/shard_map/ppermute | solution.py:44
  70.9 13.8 %collective-permute-start.16 = (bf16[8,96,384]{2,1,0:T(8,128)(2,1)}, bf16[8,96,384]{2,1,0:T(8,128)(2,1)}, u32[]{:S(2)}, u32[]{:S(2)}) collective-permute-start(bf16[8,96,384]{2,1,0:T(8,128)(2,1)} %collective-permute-done.14.refs_9_), channel_id=1, source_target_pairs={{0,8},{8,16},{16,24},{24,32},{32,40},{40,48},{48,56},{56,0},{1,9},... | collective-permute-start | bytes 1769480 | tf_op jit(solution)/shard_map/ppermute | solution.py:44
  80.5 18.8 %collective-permute-start.19 = (bf16[8,96,384]{2,1,0:T(8,128)(2,1)}, bf16[8,96,384]{2,1,0:T(8,128)(2,1)S(1)}, u32[]{:S(2)}, u32[]{:S(2)}) collective-permute-start(bf16[8,96,384]{2,1,0:T(8,128)(2,1)} %collective-permute-done.17.refs_12_), channel_id=1, source_target_pairs={{0,56},{8,0},{16,8},{24,16},{32,24},{40,32},{48,40},{56,48},{1,57}... | collective-permute-start | bytes 1769480 | tf_op jit(solution)/shard_map/ppermute | solution.py:44
  84.7 14.8 %collective-permute-start.18 = (bf16[8,96,384]{2,1,0:T(8,128)(2,1)}, bf16[8,96,384]{2,1,0:T(8,128)(2,1)S(1)}, u32[]{:S(2)}, u32[]{:S(2)}) collective-permute-start(bf16[8,96,384]{2,1,0:T(8,128)(2,1)} %collective-permute-done.16.refs_11_), channel_id=1, source_target_pairs={{0,8},{8,16},{16,24},{24,32},{32,40},{40,48},{48,56},{56,0},{1,9},... | collective-permute-start | bytes 1769480 | tf_op jit(solution)/shard_map/ppermute | solution.py:44
  86.0 21.8 %collective-permute-start.13 = (bf16[4,2,96,384]{3,2,1,0:T(8,128)(2,1)S(1)}, bf16[4,2,96,384]{3,2,1,0:T(8,128)(2,1)S(1)}, u32[]{:S(2)}, u32[]{:S(2)}) collective-permute-start(bf16[4,2,96,384]{3,2,1,0:T(8,128)(2,1)S(1)} %slice.121), channel_id=1, source_target_pairs={{0,192},{64,0},{128,64},{192,128},{1,193},{65,1},{129,65},{193,129... | collective-permute-start | bytes 1769480 | tf_op jit(solution)/shard_map/ppermute | solution.py:44
  90.6 18.1 %collective-permute-start.12 = (bf16[4,2,96,384]{3,2,1,0:T(8,128)(2,1)S(1)}, bf16[4,2,96,384]{3,2,1,0:T(8,128)(2,1)}, u32[]{:S(2)}, u32[]{:S(2)}) collective-permute-start(bf16[4,2,96,384]{3,2,1,0:T(8,128)(2,1)S(1)} %slice.120), channel_id=1, source_target_pairs={{0,64},{64,128},{128,192},{192,0},{1,65},{65,129},{129,193},{193,1... | collective-permute-start | bytes 1769480 | tf_op jit(solution)/shard_map/ppermute | solution.py:44
  90.8 10.8 %collective-permute-start.23 = (bf16[48,384]{1,0:T(8,128)(2,1)S(1)}, bf16[48,384]{1,0:T(8,128)(2,1)S(1)}, u32[]{:S(2)}, u32[]{:S(2)}) collective-permute-start(bf16[48,384]{1,0:T(8,128)(2,1)S(1)} %get-tuple-element.57), channel_id=1, source_target_pairs={{0,240},{8,248},{16,0},{24,8},{32,16},{40,24},{48,32},{56,40},{64,... | collective-permute-start | bytes 110600 | tf_op jit(solution)/shard_map/ppermute | solution.py:44
  99.4 8.4 %collective-permute-start.21 = (bf16[4,96,384]{2,1,0:T(8,128)(2,1)S(1)}, bf16[4,96,384]{2,1,0:T(8,128)(2,1)S(1)}, u32[]{:S(2)}, u32[]{:S(2)}) collective-permute-start(bf16[4,96,384]{2,1,0:T(8,128)(2,1)S(1)} %slice.123), channel_id=1, source_target_pairs={{0,56},{8,0},{16,8},{24,16},{32,24},{40,32},{48,40},{56,48},{1,57}... | collective-permute-start | bytes 884744 | tf_op jit(solution)/shard_map/ppermute | solution.py:44
  99.5 8.2 %collective-permute-start.20 = (bf16[4,96,384]{2,1,0:T(8,128)(2,1)S(1)}, bf16[4,96,384]{2,1,0:T(8,128)(2,1)S(1)}, u32[]{:S(2)}, u32[]{:S(2)}) collective-permute-start(bf16[4,96,384]{2,1,0:T(8,128)(2,1)S(1)} %slice.122), channel_id=1, source_target_pairs={{0,8},{8,16},{16,24},{24,32},{32,40},{40,48},{48,56},{56,0},{1,9},... | collective-permute-start | bytes 884744 | tf_op jit(solution)/shard_map/ppermute | solution.py:44
  101.7 6.1 %collective-permute-start.22 = (bf16[4,48,384]{2,1,0:T(8,128)(2,1)S(1)}, bf16[4,48,384]{2,1,0:T(8,128)(2,1)S(1)}, u32[]{:S(2)}, u32[]{:S(2)}) collective-permute-start(bf16[4,48,384]{2,1,0:T(8,128)(2,1)S(1)} %pad_maximum_fusion), channel_id=1, source_target_pairs={{0,248},{8,0},{16,8},{24,16},{32,24},{40,32},{48,40},{56,48},{64,5... | collective-permute-start | bytes 442376 | tf_op jit(solution)/shard_map/ppermute | solution.py:44
  137.7 14.0 %collective-permute-start.28 = (bf16[304,768]{1,0:T(8,128)(2,1)S(1)}, bf16[304,768]{1,0:T(8,128)(2,1)S(1)}, u32[]{:S(2)}, u32[]{:S(2)}) collective-permute-start(bf16[304,768]{1,0:T(8,128)(2,1)S(1)} %get-tuple-element.43), channel_id=1, source_target_pairs={{0,1},{1,2},{2,3},{3,0},{4,5},{5,6},{6,7},{7,4},{8,9},{9,10},{10,1... | collective-permute-start | bytes 1400840 | tf_op jit(solution)/shard_map/ppermute | solution.py:44
  139.2 23.3 %collective-permute-start.29 = (bf16[304,768]{1,0:T(8,128)(2,1)S(1)}, bf16[304,768]{1,0:T(8,128)(2,1)S(1)}, u32[]{:S(2)}, u32[]{:S(2)}) collective-permute-start(bf16[304,768]{1,0:T(8,128)(2,1)S(1)} %get-tuple-element.44), channel_id=1, source_target_pairs={{0,2},{1,3},{2,0},{3,1},{4,6},{5,7},{6,4},{7,5},{8,10},{9,11},{10,... | collective-permute-start | bytes 1400840 | tf_op jit(solution)/shard_map/ppermute | solution.py:44
  141.8 20.7 %collective-permute-start.30 = (bf16[304,768]{1,0:T(8,128)(2,1)S(1)}, bf16[304,768]{1,0:T(8,128)(2,1)S(1)}, u32[]{:S(2)}, u32[]{:S(2)}) collective-permute-start(bf16[304,768]{1,0:T(8,128)(2,1)S(1)} %get-tuple-element.45), channel_id=1, source_target_pairs={{0,3},{1,0},{2,1},{3,2},{4,7},{5,4},{6,5},{7,6},{8,11},{9,8},{10,9... | collective-permute-start | bytes 1400840 | tf_op jit(solution)/shard_map/ppermute | solution.py:44
  143.3 48.7 %collective-permute-start.25 = (bf16[1,48,384]{2,1,0:T(8,128)(2,1)S(1)}, bf16[1,48,384]{2,1,0:T(8,128)(2,1)S(1)}, u32[]{:S(2)}, u32[]{:S(2)}) collective-permute-start(bf16[1,48,384]{2,1,0:T(8,128)(2,1)S(1)} %copy-done.23), channel_id=1, source_target_pairs={{0,16},{8,24},{16,32},{24,40},{32,48},{40,56},{48,64},{56,72},{64,... | collective-permute-start | bytes 110600 | tf_op jit(solution)/shard_map/ppermute | solution.py:44
  145.9 46.1 %collective-permute-start.24 = (bf16[4,48,384]{2,1,0:T(8,128)(2,1)S(1)}, bf16[4,48,384]{2,1,0:T(8,128)(2,1)S(1)}, u32[]{:S(2)}, u32[]{:S(2)}) collective-permute-start(bf16[4,48,384]{2,1,0:T(8,128)(2,1)S(1)} %copy-done.21), channel_id=1, source_target_pairs={{0,8},{8,16},{16,24},{24,32},{32,40},{40,48},{48,56},{56,64},{64,7... | collective-permute-start | bytes 442376 | tf_op jit(solution)/shard_map/ppermute | solution.py:44
  165.6 11.0 %collective-permute-start.31 = (bf16[192,588]{1,0:T(8,128)(2,1)S(1)}, bf16[192,588]{1,0:T(8,128)(2,1)S(1)}, u32[]{:S(2)}, u32[]{:S(2)}) collective-permute-start(bf16[192,588]{1,0:T(8,128)(2,1)S(1)} %get-tuple-element.50), channel_id=1, source_target_pairs={{0,64},{64,128},{128,192},{192,0},{1,65},{65,129},{129,193},{193,1... | collective-permute-start | bytes 677384 | tf_op jit(solution)/shard_map/ppermute | solution.py:44
  170.2 8.9 %collective-permute-start.33 = (bf16[192,588]{1,0:T(8,128)(2,1)S(1)}, bf16[192,588]{1,0:T(8,128)(2,1)S(1)}, u32[]{:S(2)}, u32[]{:S(2)}) collective-permute-start(bf16[192,588]{1,0:T(8,128)(2,1)S(1)} %get-tuple-element.51), channel_id=1, source_target_pairs={{0,192},{64,0},{128,64},{192,128},{1,193},{65,1},{129,65},{193,129... | collective-permute-start | bytes 677384 | tf_op jit(solution)/shard_map/ppermute | solution.py:44
  170.7 11.8 %collective-permute-start.32 = (bf16[192,588]{1,0:T(8,128)(2,1)S(1)}, bf16[192,588]{1,0:T(8,128)(2,1)S(1)}, u32[]{:S(2)}, u32[]{:S(2)}) collective-permute-start(bf16[192,588]{1,0:T(8,128)(2,1)S(1)} %get-tuple-element.52), channel_id=1, source_target_pairs={{0,128},{64,192},{128,0},{192,64},{1,129},{65,193},{129,1},{193,65... | collective-permute-start | bytes 677384 | tf_op jit(solution)/shard_map/ppermute | solution.py:44
  183.3 17.6 %all-to-all-start = ((bf16[8,24,588]{2,1,0:T(8,128)(2,1)}), bf16[8,24,588]{2,1,0:T(8,128)(2,1)S(1)}, u32[]{:S(2)}, u32[]{:S(2)}) async-start(bf16[8,24,588]{2,1,0:T(8,128)(2,1)} %bitcast.32), calls=%async_computation | async-start | bytes 491520 | tf_op jit(solution)/shard_map/all_to_all | solution.py:638
  (30 other events, 311.3 us)
Sparse Core Ops, SparseCore 0:
  14.0 42.9 all-gather.3
  58.8 31.5 all-gather.5
where the time goes:
time: 211 us; the launch traced here: 208 us
  waiting for transfers between devices  74.8 us (35%)
  starting transfers between devices  74.7 us (35%)
  Pallas kernels  33.2 us (16%)
  between operations  14.5 us (7%)
  local copies, waits for them, and re-layouts  5.62 us (3%)
  other arithmetic  5.54 us (3%)
    ppermute x31, waiting for transfers between devices, ring(): return lax.ppermute(v, axis, [(i, (i + k) % n) for i in range(n)])  63.7 us
    ppermute x31, starting transfers between devices, ring(): return lax.ppermute(v, axis, [(i, (i + k) % n) for i in range(n)])  54.6 us
    pallas_call x1, Pallas kernels, layer(): pl.pallas_call(layer_kernel, out_shape=(jax.ShapeDtypeStruct((3, MOST, HW...  22.8 us
    ppermute x3, starting transfers between devices, z_swap(): return lax.ppermute(v, 'z', [(i, i ^ step) for i in range(NZ)])  11.3 us
    all_to_all x1, starting transfers between devices, per_device(): arrived = lax.all_to_all(sent, 'z', 0, 0)  8.76 us
    all_to_all x1, waiting for transfers between devices, per_device(): arrived = lax.all_to_all(sent, 'z', 0, 0)  6.49 us
    ppermute x3, waiting for transfers between devices, z_swap(): return lax.ppermute(v, 'z', [(i, i ^ step) for i in range(NZ)])  4.55 us
  transfers between devices with their start and end apart: 37, of which 23 were waited for; matrix products, arithmetic and copies ran while one was open for 3% of the time, Pallas kernels for 3%

commit v1 on v0

--- a/solution.py
+++ b/solution.py
@@ -597,15 +597,6 @@
     gain_here = jnp.where(
         c == 0, norm_gain.reshape(-1, NC, PIECE)[:, 0], norm_gain.reshape(-1, NC, PIECE)[:, 1]
     ).reshape(1, FB)
-    e_own, pix, facts = embed(place, source, got, embed_pieces, gain_here)
-    blocks = lax.all_gather(e_own, ("x", "core"), axis=0, tiled=False)
-
-    kept_cot, got_cot, bl2 = after((kept[2 * n_w :], got[2 * n_w : 2 * n_w + PACK], bl2))
-    packs = by_core(c, kept_cot[None], got_cot[None], 0)
-    packs = packs.reshape(NC, REACH, MOST, HW)
-    near = chip_shift(jnp.stack([packs[0, 1], packs[0, 2], packs[1, 2], packs[1, 3]]), -1)
-    far = chip_shift(packs[0, 3], -2)
-
     column = jnp.arange(HW, dtype=jnp.int32)[None, None, :]
     feature = (c * HC + column // HD) * (D // HEADS) + column % HD
     at = (feature // (NC * PIECE)) * PIECE + feature % PIECE
@@ -614,6 +605,15 @@
         (jnp.arange(FB, dtype=jnp.int32)[None, :, None] == at)
         & (jnp.arange(NC, dtype=jnp.int32)[:, None, None] == part)
     ).astype(BF16)
+    source, pick = after((source, pick))
+    e_own, pix, facts = embed(place, source, got, embed_pieces, gain_here)
+    blocks = lax.all_gather(e_own, ("x", "core"), axis=0, tiled=False)
+
+    kept_cot, got_cot, bl2 = after((kept[2 * n_w :], got[2 * n_w : 2 * n_w + PACK], bl2))
+    packs = by_core(c, kept_cot[None], got_cot[None], 0)
+    packs = packs.reshape(NC, REACH, MOST, HW)
+    near = chip_shift(jnp.stack([packs[0, 1], packs[0, 2], packs[1, 2], packs[1, 3]]), -1)
+    far = chip_shift(packs[0, 3], -2)
 
     att_here, att_near, att_far, own_grad, other_grad, ms = layer(
         place,

time: 211 us -> 217 us (1.028)
  waiting for transfers between devices: 74.8 us -> 84.2 us
  starting transfers between devices: 74.7 us -> 72.3 us
    ppermute x31, waiting for transfers between devices: 63.7 us -> 73.7 us  [ring(): return lax.ppermute(v, axis, [(i, (i + k) % n) for i in range(n)])]
    ppermute x31, starting transfers between devices: 54.6 us -> 50.4 us  [ring(): return lax.ppermute(v, axis, [(i, (i + k) % n) for i in range(n)])]
  transfers between devices with their start and end apart: 37 -> 37, of which waited for: 23 -> 23; matrix products, arithmetic and copies ran while one was open for 3% -> 2% of each run, Pallas kernels for 3% -> 3%
where the time goes in v1:
time: 217 us; the launch traced here: 214 us
  waiting for transfers between devices  84.2 us (39%)
  starting transfers between devices  72.3 us (33%)
  Pallas kernels  33 us (15%)
  between operations  14.5 us (7%)
  other arithmetic  5.58 us (3%)
  local copies, waits for them, and re-layouts  4.62 us (2%)
    ppermute x31, waiting for transfers between devices, ring(): return lax.ppermute(v, axis, [(i, (i + k) % n) for i in range(n)])  73.7 us
    ppermute x31, starting transfers between devices, ring(): return lax.ppermute(v, axis, [(i, (i + k) % n) for i in range(n)])  50.4 us
    pallas_call x1, Pallas kernels, layer(): pl.pallas_call(layer_kernel, out_shape=(jax.ShapeDtypeStruct((3, MOST, HW...  22.5 us
    ppermute x3, starting transfers between devices, z_swap(): return lax.ppermute(v, 'z', [(i, i ^ step) for i in range(NZ)])  11.3 us
    all_to_all x1, starting transfers between devices, per_device(): arrived = lax.all_to_all(sent, 'z', 0, 0)  10.5 us
    all_to_all x1, waiting for transfers between devices, per_device(): arrived = lax.all_to_all(sent, 'z', 0, 0)  6.49 us
  transfers between devices with their start and end apart: 37, of which 23 were waited for; matrix products, arithmetic and copies ran while one was open for 2% of the time, Pallas kernels for 3%

profile of v1, /device:TPU:32, one launch (start us, length us, event | category | flops | bytes accessed | tf_op | source)
XLA Modules:
  0.0 214.3 jit_solution(2396882765832460088)
XLA Ops:
  7.9 3.0 %prep.1 = (bf16[672,384]{1,0:T(8,128)(2,1)}, bf16[384,384]{1,0:T(8,128)(2,1)}, bf16[144,768]{1,0:T(8,128)(2,1)}) custom-call(s32[4]{0:T(128)} %pad_add_fusion.place.refs_0_, s32[3]{0:T(128)} %counts.1, s32[3]{0:T(128)} %packs.1, bf16[96,768]{1,0:T(8,128)(2,1)} %wq_in.1, bf16[96,768]{1,0:T(8,128)(2,1)} %wk_in.1, bf16[192,768]{1,0:T(8,128)(2,1)} %cot_in.1, ...), custom_call_target="tpu_custom_call" | custom-call | flops 1000000 | bytes 2000000 | tf_op jit(solution)/shard_map/prep/pallas_call | solution.py:139
  14.0 1.9 collective-permute-start.1
  16.2 1.8 collective-permute-done.1
  18.0 3.4 %collective-permute-start.2 = (bf16[48,588]{1,0:T(8,128)(2,1)S(1)}, bf16[48,588]{1,0:T(8,128)(2,1)S(1)}, u32[]{:S(2)}, u32[]{:S(2)}) collective-permute-start(bf16[48,588]{1,0:T(8,128)(2,1)S(1)} %maximum_select_fusion.6), channel_id=1, source_target_pairs={{0,16},{8,24},{16,0},{24,8},{32,48},{40,56},{48,32},{56,40},{1,17}... | collective-permute-start | bytes 169352 | tf_op jit(solution)/shard_map/ppermute | solution.py:56
  21.5 2.1 %collective-permute-done.2 = bf16[48,588]{1,0:T(8,128)(2,1)S(1)} collective-permute-done((bf16[48,588]{1,0:T(8,128)(2,1)S(1)}, bf16[48,588]{1,0:T(8,128)(2,1)S(1)}, u32[]{:S(2)}, u32[]{:S(2)}) %collective-permute-start.2) | collective-permute-done | bytes 56480 | tf_op jit(solution)/shard_map/ppermute | solution.py:56
  23.7 6.1 %collective-permute-start.3 = (bf16[96,588]{1,0:T(8,128)(2,1)S(1)}, bf16[96,588]{1,0:T(8,128)(2,1)S(1)}, u32[]{:S(2)}, u32[]{:S(2)}) collective-permute-start(bf16[96,588]{1,0:T(8,128)(2,1)S(1)} %maximum_select_fusion.5), channel_id=1, source_target_pairs={{0,32},{8,40},{16,48},{24,56},{32,0},{40,8},{48,16},{56,24},{1,33}... | collective-permute-start | bytes 338696 | tf_op jit(solution)/shard_map/ppermute | solution.py:56
  31.4 2.9 %collective-permute-start.5 = (bf16[2,96,384]{2,1,0:T(8,128)(2,1)S(1)}, bf16[2,96,384]{2,1,0:T(8,128)(2,1)S(1)}, u32[]{:S(2)}, u32[]{:S(2)}) collective-permute-start(bf16[2,96,384]{2,1,0:T(8,128)(2,1)S(1)} %maximum_select_fusion.3.refs_0_), channel_id=1, source_target_pairs={{0,128},{64,192},{128,0},{192,64},{1,129},{65,193},{129,1},{193,65... | collective-permute-start | bytes 442376 | tf_op jit(solution)/shard_map/ppermute | solution.py:44
  37.2 1.8 collective-permute-done.5.refs_2_
  40.7 2.8 %collective-permute-start.8 = (bf16[192,588]{1,0:T(8,128)(2,1)S(1)}, bf16[192,588]{1,0:T(8,128)(2,1)S(1)}, u32[]{:S(2)}, u32[]{:S(2)}) collective-permute-start(bf16[192,588]{1,0:T(8,128)(2,1)S(1)} %maximum_select_fusion.2.w0), channel_id=1, source_target_pairs={{0,128},{64,192},{128,0},{192,64},{1,129},{65,193},{129,1},{193,65... | collective-permute-start | bytes 677384 | tf_op jit(solution)/shard_map/ppermute | solution.py:44
  45.8 2.0 collective-permute-done.9.w3
  47.8 2.6 %collective-permute-done.8.w2 = bf16[192,588]{1,0:T(8,128)(2,1)S(1)} collective-permute-done((bf16[192,588]{1,0:T(8,128)(2,1)S(1)}, bf16[192,588]{1,0:T(8,128)(2,1)S(1)}, u32[]{:S(2)}, u32[]{:S(2)}) %collective-permute-start.8) | collective-permute-done | bytes 225824 | tf_op jit(solution)/shard_map/ppermute | solution.py:44
  50.6 2.0 embed.1
  53.3 2.1 order.1.refs_8_
  57.4 2.7 %collective-permute-start.11 = (bf16[8,2,96,384]{3,2,1,0:T(8,128)(2,1)}, bf16[8,2,96,384]{3,2,1,0:T(8,128)(2,1)S(1)}, u32[]{:S(2)}, u32[]{:S(2)}) collective-permute-start(bf16[8,2,96,384]{3,2,1,0:T(8,128)(2,1)} %all-gather.4.cloned.1.call-done.refs_3_), channel_id=1, source_target_pairs={{0,192},{64,0},{128,64},{192,128},{1,193},{65,1},{129,65},{193,129... | collective-permute-start | bytes 3538952 | tf_op jit(solution)/shard_map/ppermute | solution.py:44
  60.0 8.8 %collective-permute-done.15.refs_10_ = bf16[8,96,384]{2,1,0:T(8,128)(2,1)} collective-permute-done((bf16[8,96,384]{2,1,0:T(8,128)(2,1)}, bf16[8,96,384]{2,1,0:T(8,128)(2,1)}, u32[]{:S(2)}, u32[]{:S(2)}) %collective-permute-start.15) | collective-permute-done | bytes 589856 | tf_op jit(solution)/shard_map/ppermute | solution.py:44
  71.0 9.7 %collective-permute-done.17.refs_12_ = bf16[8,96,384]{2,1,0:T(8,128)(2,1)S(1)} collective-permute-done((bf16[8,96,384]{2,1,0:T(8,128)(2,1)}, bf16[8,96,384]{2,1,0:T(8,128)(2,1)S(1)}, u32[]{:S(2)}, u32[]{:S(2)}) %collective-permute-start.17) | collective-permute-done | bytes 589856 | tf_op jit(solution)/shard_map/ppermute | solution.py:44
  80.6 3.7 %collective-permute-start.19 = (bf16[8,96,384]{2,1,0:T(8,128)(2,1)S(1)}, bf16[8,96,384]{2,1,0:T(8,128)(2,1)S(1)}, u32[]{:S(2)}, u32[]{:S(2)}) collective-permute-start(bf16[8,96,384]{2,1,0:T(8,128)(2,1)S(1)} %collective-permute-done.17.refs_12_), channel_id=1, source_target_pairs={{0,56},{8,0},{16,8},{24,16},{32,24},{40,32},{48,40},{56,48},{1,57}... | collective-permute-start | bytes 1769480 | tf_op jit(solution)/shard_map/ppermute | solution.py:44
  84.8 4.5 %collective-permute-start.13 = (bf16[4,2,96,384]{3,2,1,0:T(8,128)(2,1)S(1)}, bf16[4,2,96,384]{3,2,1,0:T(8,128)(2,1)S(1)}, u32[]{:S(2)}, u32[]{:S(2)}) collective-permute-start(bf16[4,2,96,384]{3,2,1,0:T(8,128)(2,1)S(1)} %slice.121), channel_id=1, source_target_pairs={{0,192},{64,0},{128,64},{192,128},{1,193},{65,1},{129,65},{193,129... | collective-permute-start | bytes 1769480 | tf_op jit(solution)/shard_map/ppermute | solution.py:44
  89.8 4.1 %collective-permute-done.19.refs_14_ = bf16[8,96,384]{2,1,0:T(8,128)(2,1)S(1)} collective-permute-done((bf16[8,96,384]{2,1,0:T(8,128)(2,1)S(1)}, bf16[8,96,384]{2,1,0:T(8,128)(2,1)S(1)}, u32[]{:S(2)}, u32[]{:S(2)}) %collective-permute-start.19) | collective-permute-done | bytes 589856 | tf_op jit(solution)/shard_map/ppermute | solution.py:44
  93.9 3.8 %collective-permute-start.21 = (bf16[4,96,384]{2,1,0:T(8,128)(2,1)S(1)}, bf16[4,96,384]{2,1,0:T(8,128)(2,1)S(1)}, u32[]{:S(2)}, u32[]{:S(2)}) collective-permute-start(bf16[4,96,384]{2,1,0:T(8,128)(2,1)S(1)} %slice.123), channel_id=1, source_target_pairs={{0,56},{8,0},{16,8},{24,16},{32,24},{40,32},{48,40},{56,48},{1,57}... | collective-permute-start | bytes 884744 | tf_op jit(solution)/shard_map/ppermute | solution.py:44
  98.1 10.5 %collective-permute-start.23 = (bf16[48,384]{1,0:T(8,128)(2,1)S(1)}, bf16[48,384]{1,0:T(8,128)(2,1)S(1)}, u32[]{:S(2)}, u32[]{:S(2)}) collective-permute-start(bf16[48,384]{1,0:T(8,128)(2,1)S(1)} %get-tuple-element.61), channel_id=1, source_target_pairs={{0,240},{8,248},{16,0},{24,8},{32,16},{40,24},{48,32},{56,40},{64,... | collective-permute-start | bytes 110600 | tf_op jit(solution)/shard_map/ppermute | solution.py:44
  110.3 5.1 %collective-permute-done.22.refs_19_ = bf16[4,48,384]{2,1,0:T(8,128)(2,1)S(1)} collective-permute-done((bf16[4,48,384]{2,1,0:T(8,128)(2,1)S(1)}, bf16[4,48,384]{2,1,0:T(8,128)(2,1)S(1)}, u32[]{:S(2)}, u32[]{:S(2)}) %collective-permute-start.22) | collective-permute-done | bytes 147488 | tf_op jit(solution)/shard_map/ppermute | solution.py:44
  116.4 22.5 %layer.1 = (bf16[3,48,384]{2,1,0:T(8,128)(2,1)}, bf16[4,48,384]{2,1,0:T(8,128)(2,1)}, bf16[1,48,384]{2,1,0:T(8,128)(2,1)}, bf16[4,304,768]{2,1,0:T(8,128)(2,1)},...) custom-call(s32[4]{0:T(128)} %pad_add_fusion.place.refs_0_, s32[8,128]{1,0:T(8,128)} %copy-done.6, ...), custom_call_target="tpu_custom_call" | custom-call | flops 5435817984 | bytes 20000000 | tf_op jit(solution)/shard_map/layer/pallas_call | solution.py:449
  139.1 4.0 %collective-permute-done.27.got = bf16[4,304,768]{2,1,0:T(8,128)(2,1)S(1)} collective-permute-done((bf16[4,304,768]{2,1,0:T(8,128)(2,1)}, bf16[4,304,768]{2,1,0:T(8,128)(2,1)S(1)}, u32[]{:S(2)}, u32[]{:S(2)}) %collective-permute-start.27) | collective-permute-done | bytes 1867808 | tf_op jit(solution)/shard_map/ppermute | solution.py:44
  146.5 2.7 %collective-permute-start.29 = (bf16[304,768]{1,0:T(8,128)(2,1)S(1)}, bf16[304,768]{1,0:T(8,128)(2,1)S(1)}, u32[]{:S(2)}, u32[]{:S(2)}) collective-permute-start(bf16[304,768]{1,0:T(8,128)(2,1)S(1)} %get-tuple-element.48), channel_id=1, source_target_pairs={{0,2},{1,3},{2,0},{3,1},{4,6},{5,7},{6,4},{7,5},{8,10},{9,11},{10,... | collective-permute-start | bytes 1400840 | tf_op jit(solution)/shard_map/ppermute | solution.py:44
  151.1 8.1 %collective-permute-done.28.r1 = bf16[304,768]{1,0:T(8,128)(2,1)S(1)} collective-permute-done((bf16[304,768]{1,0:T(8,128)(2,1)S(1)}, bf16[304,768]{1,0:T(8,128)(2,1)S(1)}, u32[]{:S(2)}, u32[]{:S(2)}) %collective-permute-start.28) | collective-permute-done | bytes 466976 | tf_op jit(solution)/shard_map/ppermute | solution.py:44
  159.2 10.7 %collective-permute-done.29.r2 = bf16[304,768]{1,0:T(8,128)(2,1)S(1)} collective-permute-done((bf16[304,768]{1,0:T(8,128)(2,1)S(1)}, bf16[304,768]{1,0:T(8,128)(2,1)S(1)}, u32[]{:S(2)}, u32[]{:S(2)}) %collective-permute-start.29) | collective-permute-done | bytes 466976 | tf_op jit(solution)/shard_map/ppermute | solution.py:44
  169.9 2.9 %embed_back.1 = (f32[192,588]{1,0:T(8,128)S(1)}, bf16[3,192,588]{2,1,0:T(8,128)(2,1)S(1)}) custom-call(s32[4]{0:T(128)S(1)} %copy-done.5, bf16[304,768]{1,0:T(8,128)(2,1)S(1)} %get-tuple-element.46.own, bf16[304,768]{1,0:T(8,128)(2,1)S(1)} %collective-permute-done.28.r1, bf16[304,768]{1,0:T(8,128)(2,1)S(1)} %collective-permute-done.29.r2, ...), custom_call_target="tpu_custom_call" | custom-call | flops 260112384 | bytes 5000000 | tf_op jit(solution)/shard_map/embed_back/pallas_call | solution.py:534
  173.0 3.2 %collective-permute-start.33 = (bf16[192,588]{1,0:T(8,128)(2,1)S(1)}, bf16[192,588]{1,0:T(8,128)(2,1)S(1)}, u32[]{:S(2)}, u32[]{:S(2)}) collective-permute-start(bf16[192,588]{1,0:T(8,128)(2,1)S(1)} %get-tuple-element.55), channel_id=1, source_target_pairs={{0,192},{64,0},{128,64},{192,128},{1,193},{65,1},{129,65},{193,129... | collective-permute-start | bytes 677384 | tf_op jit(solution)/shard_map/ppermute | solution.py:44
  176.9 9.7 %collective-permute-done.31 = bf16[192,588]{1,0:T(8,128)(2,1)S(1)} collective-permute-done((bf16[192,588]{1,0:T(8,128)(2,1)S(1)}, bf16[192,588]{1,0:T(8,128)(2,1)S(1)}, u32[]{:S(2)}, u32[]{:S(2)}) %collective-permute-start.31) | collective-permute-done | bytes 225824 | tf_op jit(solution)/shard_map/ppermute | solution.py:44
  187.4 10.5 %all-to-all-start = ((bf16[8,24,588]{2,1,0:T(8,128)(2,1)}), bf16[8,24,588]{2,1,0:T(8,128)(2,1)S(1)}, u32[]{:S(2)}, u32[]{:S(2)}) async-start(bf16[8,24,588]{2,1,0:T(8,128)(2,1)} %bitcast.32), calls=%async_computation | async-start | bytes 491520 | tf_op jit(solution)/shard_map/all_to_all | solution.py:638
  200.3 6.5 %all-to-all-done = bf16[8,24,588]{2,1,0:T(8,128)(2,1)S(1)} async-done(((bf16[8,24,588]{2,1,0:T(8,128)(2,1)}), bf16[8,24,588]{2,1,0:T(8,128)(2,1)S(1)}, u32[]{:S(2)}, u32[]{:S(2)}) %all-to-all-start) | async-done | bytes 225824 | tf_op jit(solution)/shard_map/all_to_all | solution.py:638
  (140 shorter events, 31.5 us)
Async XLA Ops:
  7.2 50.2 %all-gather.4.cloned.1.call-start = ((), (), s32[]{:S(2)}) async-start(), calls=%async_computation.1 | async-start | bytes 1327104 | tf_op jit(solution)/shard_map/all_gather | solution.py:582
  14.0 102.4 %all-gather.6.cloned.1.call-start = ((), (), s32[]{:S(2)}) async-start(), calls=%async_computation.2 | async-start | bytes 4202496 | tf_op jit(solution)/shard_map/all_gather | solution.py:610
  18.0 5.6 %collective-permute-start.2 = (bf16[48,588]{1,0:T(8,128)(2,1)S(1)}, bf16[48,588]{1,0:T(8,128)(2,1)S(1)}, u32[]{:S(2)}, u32[]{:S(2)}) collective-permute-start(bf16[48,588]{1,0:T(8,128)(2,1)S(1)} %maximum_select_fusion.6), channel_id=1, source_target_pairs={{0,16},{8,24},{16,0},{24,8},{32,48},{40,56},{48,32},{56,40},{1,17}... | collective-permute-start | bytes 169352 | tf_op jit(solution)/shard_map/ppermute | solution.py:56
  23.7 12.2 %collective-permute-start.3 = (bf16[96,588]{1,0:T(8,128)(2,1)S(1)}, bf16[96,588]{1,0:T(8,128)(2,1)S(1)}, u32[]{:S(2)}, u32[]{:S(2)}) collective-permute-start(bf16[96,588]{1,0:T(8,128)(2,1)S(1)} %maximum_select_fusion.5), channel_id=1, source_target_pairs={{0,32},{8,40},{16,48},{24,56},{32,0},{40,8},{48,16},{56,24},{1,33}... | collective-permute-start | bytes 338696 | tf_op jit(solution)/shard_map/ppermute | solution.py:56
  29.8 7.4 %collective-permute-start.6 = (bf16[2,96,384]{2,1,0:T(8,128)(2,1)S(1)}, bf16[2,96,384]{2,1,0:T(8,128)(2,1)S(1)}, u32[]{:S(2)}, u32[]{:S(2)}) collective-permute-start(bf16[2,96,384]{2,1,0:T(8,128)(2,1)S(1)} %maximum_select_fusion.3.refs_0_), channel_id=1, source_target_pairs={{0,64},{64,128},{128,192},{192,0},{1,65},{65,129},{129,193},{193,1... | collective-permute-start | bytes 442376 | tf_op jit(solution)/shard_map/ppermute | solution.py:44
  31.4 7.6 %collective-permute-start.5 = (bf16[2,96,384]{2,1,0:T(8,128)(2,1)S(1)}, bf16[2,96,384]{2,1,0:T(8,128)(2,1)S(1)}, u32[]{:S(2)}, u32[]{:S(2)}) collective-permute-start(bf16[2,96,384]{2,1,0:T(8,128)(2,1)S(1)} %maximum_select_fusion.3.refs_0_), channel_id=1, source_target_pairs={{0,128},{64,192},{128,0},{192,64},{1,129},{65,193},{129,1},{193,65... | collective-permute-start | bytes 442376 | tf_op jit(solution)/shard_map/ppermute | solution.py:44
  39.5 8.3 %collective-permute-start.9 = (bf16[192,588]{1,0:T(8,128)(2,1)S(1)}, bf16[192,588]{1,0:T(8,128)(2,1)S(1)}, u32[]{:S(2)}, u32[]{:S(2)}) collective-permute-start(bf16[192,588]{1,0:T(8,128)(2,1)S(1)} %maximum_select_fusion.2.w0), channel_id=1, source_target_pairs={{0,64},{64,128},{128,192},{192,0},{1,65},{65,129},{129,193},{193,1... | collective-permute-start | bytes 677384 | tf_op jit(solution)/shard_map/ppermute | solution.py:44
  40.7 9.8 %collective-permute-start.8 = (bf16[192,588]{1,0:T(8,128)(2,1)S(1)}, bf16[192,588]{1,0:T(8,128)(2,1)S(1)}, u32[]{:S(2)}, u32[]{:S(2)}) collective-permute-start(bf16[192,588]{1,0:T(8,128)(2,1)S(1)} %maximum_select_fusion.2.w0), channel_id=1, source_target_pairs={{0,128},{64,192},{128,0},{192,64},{1,129},{65,193},{129,1},{193,65... | collective-permute-start | bytes 677384 | tf_op jit(solution)/shard_map/ppermute | solution.py:44
  43.5 7.1 %collective-permute-start.7 = (bf16[192,588]{1,0:T(8,128)(2,1)S(1)}, bf16[192,588]{1,0:T(8,128)(2,1)S(1)}, u32[]{:S(2)}, u32[]{:S(2)}) collective-permute-start(bf16[192,588]{1,0:T(8,128)(2,1)S(1)} %maximum_select_fusion.2.w0), channel_id=1, source_target_pairs={{0,192},{64,0},{128,64},{192,128},{1,193},{65,1},{129,65},{193,129... | collective-permute-start | bytes 677384 | tf_op jit(solution)/shard_map/ppermute | solution.py:44
  55.3 13.5 %collective-permute-start.15 = (bf16[8,96,384]{2,1,0:T(8,128)(2,1)}, bf16[8,96,384]{2,1,0:T(8,128)(2,1)}, u32[]{:S(2)}, u32[]{:S(2)}) collective-permute-start(bf16[8,96,384]{2,1,0:T(8,128)(2,1)} %order.1.refs_8_), channel_id=1, source_target_pairs={{0,56},{8,0},{16,8},{24,16},{32,24},{40,32},{48,40},{56,48},{1,57}... | collective-permute-start | bytes 1769480 | tf_op jit(solution)/shard_map/ppermute | solution.py:44
  57.1 13.9 %collective-permute-start.14 = (bf16[8,96,384]{2,1,0:T(8,128)(2,1)}, bf16[8,96,384]{2,1,0:T(8,128)(2,1)}, u32[]{:S(2)}, u32[]{:S(2)}) collective-permute-start(bf16[8,96,384]{2,1,0:T(8,128)(2,1)} %order.1.refs_8_), channel_id=1, source_target_pairs={{0,8},{8,16},{16,24},{24,32},{32,40},{40,48},{48,56},{56,0},{1,9},... | collective-permute-start | bytes 1769480 | tf_op jit(solution)/shard_map/ppermute | solution.py:44
  57.4 27.4 %collective-permute-start.11 = (bf16[8,2,96,384]{3,2,1,0:T(8,128)(2,1)}, bf16[8,2,96,384]{3,2,1,0:T(8,128)(2,1)S(1)}, u32[]{:S(2)}, u32[]{:S(2)}) collective-permute-start(bf16[8,2,96,384]{3,2,1,0:T(8,128)(2,1)} %all-gather.4.cloned.1.call-done.refs_3_), channel_id=1, source_target_pairs={{0,192},{64,0},{128,64},{192,128},{1,193},{65,1},{129,65},{193,129... | collective-permute-start | bytes 3538952 | tf_op jit(solution)/shard_map/ppermute | solution.py:44
  60.0 29.3 %collective-permute-start.10 = (bf16[8,2,96,384]{3,2,1,0:T(8,128)(2,1)}, bf16[8,2,96,384]{3,2,1,0:T(8,128)(2,1)S(1)}, u32[]{:S(2)}, u32[]{:S(2)}) collective-permute-start(bf16[8,2,96,384]{3,2,1,0:T(8,128)(2,1)} %all-gather.4.cloned.1.call-done.refs_3_), channel_id=1, source_target_pairs={{0,64},{64,128},{128,192},{192,0},{1,65},{65,129},{129,193},{193,1... | collective-permute-start | bytes 3538952 | tf_op jit(solution)/shard_map/ppermute | solution.py:44
  68.8 11.8 %collective-permute-start.17 = (bf16[8,96,384]{2,1,0:T(8,128)(2,1)}, bf16[8,96,384]{2,1,0:T(8,128)(2,1)S(1)}, u32[]{:S(2)}, u32[]{:S(2)}) collective-permute-start(bf16[8,96,384]{2,1,0:T(8,128)(2,1)} %collective-permute-done.15.refs_10_), channel_id=1, source_target_pairs={{0,56},{8,0},{16,8},{24,16},{32,24},{40,32},{48,40},{56,48},{1,57}... | collective-permute-start | bytes 1769480 | tf_op jit(solution)/shard_map/ppermute | solution.py:44
  71.0 13.7 %collective-permute-start.16 = (bf16[8,96,384]{2,1,0:T(8,128)(2,1)}, bf16[8,96,384]{2,1,0:T(8,128)(2,1)S(1)}, u32[]{:S(2)}, u32[]{:S(2)}) collective-permute-start(bf16[8,96,384]{2,1,0:T(8,128)(2,1)} %collective-permute-done.14.refs_9_), channel_id=1, source_target_pairs={{0,8},{8,16},{16,24},{24,32},{32,40},{40,48},{48,56},{56,0},{1,9},... | collective-permute-start | bytes 1769480 | tf_op jit(solution)/shard_map/ppermute | solution.py:44
  80.6 13.3 %collective-permute-start.19 = (bf16[8,96,384]{2,1,0:T(8,128)(2,1)S(1)}, bf16[8,96,384]{2,1,0:T(8,128)(2,1)S(1)}, u32[]{:S(2)}, u32[]{:S(2)}) collective-permute-start(bf16[8,96,384]{2,1,0:T(8,128)(2,1)S(1)} %collective-permute-done.17.refs_12_), channel_id=1, source_target_pairs={{0,56},{8,0},{16,8},{24,16},{32,24},{40,32},{48,40},{56,48},{1,57}... | collective-permute-start | bytes 1769480 | tf_op jit(solution)/shard_map/ppermute | solution.py:44
  84.7 13.3 %collective-permute-start.18 = (bf16[8,96,384]{2,1,0:T(8,128)(2,1)S(1)}, bf16[8,96,384]{2,1,0:T(8,128)(2,1)S(1)}, u32[]{:S(2)}, u32[]{:S(2)}) collective-permute-start(bf16[8,96,384]{2,1,0:T(8,128)(2,1)S(1)} %collective-permute-done.16.refs_11_), channel_id=1, source_target_pairs={{0,8},{8,16},{16,24},{24,32},{32,40},{40,48},{48,56},{56,0},{1,9},... | collective-permute-start | bytes 1769480 | tf_op jit(solution)/shard_map/ppermute | solution.py:44
  84.8 30.6 %collective-permute-start.13 = (bf16[4,2,96,384]{3,2,1,0:T(8,128)(2,1)S(1)}, bf16[4,2,96,384]{3,2,1,0:T(8,128)(2,1)S(1)}, u32[]{:S(2)}, u32[]{:S(2)}) collective-permute-start(bf16[4,2,96,384]{3,2,1,0:T(8,128)(2,1)S(1)} %slice.121), channel_id=1, source_target_pairs={{0,192},{64,0},{128,64},{192,128},{1,193},{65,1},{129,65},{193,129... | collective-permute-start | bytes 1769480 | tf_op jit(solution)/shard_map/ppermute | solution.py:44
  89.4 26.9 %collective-permute-start.12 = (bf16[4,2,96,384]{3,2,1,0:T(8,128)(2,1)S(1)}, bf16[4,2,96,384]{3,2,1,0:T(8,128)(2,1)}, u32[]{:S(2)}, u32[]{:S(2)}) collective-permute-start(bf16[4,2,96,384]{3,2,1,0:T(8,128)(2,1)S(1)} %slice.120), channel_id=1, source_target_pairs={{0,64},{64,128},{128,192},{192,0},{1,65},{65,129},{129,193},{193,1... | collective-permute-start | bytes 1769480 | tf_op jit(solution)/shard_map/ppermute | solution.py:44
  93.9 21.5 %collective-permute-start.21 = (bf16[4,96,384]{2,1,0:T(8,128)(2,1)S(1)}, bf16[4,96,384]{2,1,0:T(8,128)(2,1)S(1)}, u32[]{:S(2)}, u32[]{:S(2)}) collective-permute-start(bf16[4,96,384]{2,1,0:T(8,128)(2,1)S(1)} %slice.123), channel_id=1, source_target_pairs={{0,56},{8,0},{16,8},{24,16},{32,24},{40,32},{48,40},{56,48},{1,57}... | collective-permute-start | bytes 884744 | tf_op jit(solution)/shard_map/ppermute | solution.py:44
  98.0 17.4 %collective-permute-start.20 = (bf16[4,96,384]{2,1,0:T(8,128)(2,1)S(1)}, bf16[4,96,384]{2,1,0:T(8,128)(2,1)S(1)}, u32[]{:S(2)}, u32[]{:S(2)}) collective-permute-start(bf16[4,96,384]{2,1,0:T(8,128)(2,1)S(1)} %slice.122), channel_id=1, source_target_pairs={{0,8},{8,16},{16,24},{24,32},{32,40},{40,48},{48,56},{56,0},{1,9},... | collective-permute-start | bytes 884744 | tf_op jit(solution)/shard_map/ppermute | solution.py:44
  98.1 12.1 %collective-permute-start.23 = (bf16[48,384]{1,0:T(8,128)(2,1)S(1)}, bf16[48,384]{1,0:T(8,128)(2,1)S(1)}, u32[]{:S(2)}, u32[]{:S(2)}) collective-permute-start(bf16[48,384]{1,0:T(8,128)(2,1)S(1)} %get-tuple-element.61), channel_id=1, source_target_pairs={{0,240},{8,248},{16,0},{24,8},{32,16},{40,24},{48,32},{56,40},{64,... | collective-permute-start | bytes 110600 | tf_op jit(solution)/shard_map/ppermute | solution.py:44
  110.3 5.1 %collective-permute-start.22 = (bf16[4,48,384]{2,1,0:T(8,128)(2,1)S(1)}, bf16[4,48,384]{2,1,0:T(8,128)(2,1)S(1)}, u32[]{:S(2)}, u32[]{:S(2)}) collective-permute-start(bf16[4,48,384]{2,1,0:T(8,128)(2,1)S(1)} %pad_maximum_fusion), channel_id=1, source_target_pairs={{0,248},{8,0},{16,8},{24,16},{32,24},{40,32},{48,40},{56,48},{64,5... | collective-permute-start | bytes 442376 | tf_op jit(solution)/shard_map/ppermute | solution.py:44
  145.1 14.1 %collective-permute-start.28 = (bf16[304,768]{1,0:T(8,128)(2,1)S(1)}, bf16[304,768]{1,0:T(8,128)(2,1)S(1)}, u32[]{:S(2)}, u32[]{:S(2)}) collective-permute-start(bf16[304,768]{1,0:T(8,128)(2,1)S(1)} %get-tuple-element.47), channel_id=1, source_target_pairs={{0,1},{1,2},{2,3},{3,0},{4,5},{5,6},{6,7},{7,4},{8,9},{9,10},{10,1... | collective-permute-start | bytes 1400840 | tf_op jit(solution)/shard_map/ppermute | solution.py:44
  146.5 23.4 %collective-permute-start.29 = (bf16[304,768]{1,0:T(8,128)(2,1)S(1)}, bf16[304,768]{1,0:T(8,128)(2,1)S(1)}, u32[]{:S(2)}, u32[]{:S(2)}) collective-permute-start(bf16[304,768]{1,0:T(8,128)(2,1)S(1)} %get-tuple-element.48), channel_id=1, source_target_pairs={{0,2},{1,3},{2,0},{3,1},{4,6},{5,7},{6,4},{7,5},{8,10},{9,11},{10,... | collective-permute-start | bytes 1400840 | tf_op jit(solution)/shard_map/ppermute | solution.py:44
  149.2 20.7 %collective-permute-start.30 = (bf16[304,768]{1,0:T(8,128)(2,1)S(1)}, bf16[304,768]{1,0:T(8,128)(2,1)S(1)}, u32[]{:S(2)}, u32[]{:S(2)}) collective-permute-start(bf16[304,768]{1,0:T(8,128)(2,1)S(1)} %get-tuple-element.49), channel_id=1, source_target_pairs={{0,3},{1,0},{2,1},{3,2},{4,7},{5,4},{6,5},{7,6},{8,11},{9,8},{10,9... | collective-permute-start | bytes 1400840 | tf_op jit(solution)/shard_map/ppermute | solution.py:44
  150.8 47.2 %collective-permute-start.25 = (bf16[1,48,384]{2,1,0:T(8,128)(2,1)S(1)}, bf16[1,48,384]{2,1,0:T(8,128)(2,1)S(1)}, u32[]{:S(2)}, u32[]{:S(2)}) collective-permute-start(bf16[1,48,384]{2,1,0:T(8,128)(2,1)S(1)} %copy-done.27), channel_id=1, source_target_pairs={{0,16},{8,24},{16,32},{24,40},{32,48},{40,56},{48,64},{56,72},{64,... | collective-permute-start | bytes 110600 | tf_op jit(solution)/shard_map/ppermute | solution.py:44
  151.0 46.9 %collective-permute-start.24 = (bf16[4,48,384]{2,1,0:T(8,128)(2,1)S(1)}, bf16[4,48,384]{2,1,0:T(8,128)(2,1)S(1)}, u32[]{:S(2)}, u32[]{:S(2)}) collective-permute-start(bf16[4,48,384]{2,1,0:T(8,128)(2,1)S(1)} %copy-done.25), channel_id=1, source_target_pairs={{0,8},{8,16},{16,24},{24,32},{32,40},{40,48},{48,56},{56,64},{64,7... | collective-permute-start | bytes 442376 | tf_op jit(solution)/shard_map/ppermute | solution.py:44
  172.9 13.7 %collective-permute-start.31 = (bf16[192,588]{1,0:T(8,128)(2,1)S(1)}, bf16[192,588]{1,0:T(8,128)(2,1)S(1)}, u32[]{:S(2)}, u32[]{:S(2)}) collective-permute-start(bf16[192,588]{1,0:T(8,128)(2,1)S(1)} %get-tuple-element.54), channel_id=1, source_target_pairs={{0,64},{64,128},{128,192},{192,0},{1,65},{65,129},{129,193},{193,1... | collective-permute-start | bytes 677384 | tf_op jit(solution)/shard_map/ppermute | solution.py:44
  173.0 13.6 %collective-permute-start.33 = (bf16[192,588]{1,0:T(8,128)(2,1)S(1)}, bf16[192,588]{1,0:T(8,128)(2,1)S(1)}, u32[]{:S(2)}, u32[]{:S(2)}) collective-permute-start(bf16[192,588]{1,0:T(8,128)(2,1)S(1)} %get-tuple-element.55), channel_id=1, source_target_pairs={{0,192},{64,0},{128,64},{192,128},{1,193},{65,1},{129,65},{193,129... | collective-permute-start | bytes 677384 | tf_op jit(solution)/shard_map/ppermute | solution.py:44
  176.2 10.4 %collective-permute-start.32 = (bf16[192,588]{1,0:T(8,128)(2,1)S(1)}, bf16[192,588]{1,0:T(8,128)(2,1)S(1)}, u32[]{:S(2)}, u32[]{:S(2)}) collective-permute-start(bf16[192,588]{1,0:T(8,128)(2,1)S(1)} %get-tuple-element.56), channel_id=1, source_target_pairs={{0,128},{64,192},{128,0},{192,64},{1,129},{65,193},{129,1},{193,65... | collective-permute-start | bytes 677384 | tf_op jit(solution)/shard_map/ppermute | solution.py:44
  187.4 19.3 %all-to-all-start = ((bf16[8,24,588]{2,1,0:T(8,128)(2,1)}), bf16[8,24,588]{2,1,0:T(8,128)(2,1)S(1)}, u32[]{:S(2)}, u32[]{:S(2)}) async-start(bf16[8,24,588]{2,1,0:T(8,128)(2,1)} %bitcast.32), calls=%async_computation | async-start | bytes 491520 | tf_op jit(solution)/shard_map/all_to_all | solution.py:638
  (35 other events, 420.4 us)
Sparse Core Ops, SparseCore 0:
  14.1 42.9 all-gather.3
  58.9 31.5 all-gather.5
